TPU v7x, 32 devices: a whole 2x2x4 slice. The times are simulated.
32 devices in a mesh: dp: 2 (over x), ctx: 4 (over y, core), tensor: 4 (over z).
Axes of the slice: x: 2, y: 2, z: 4, core: 2. Of those that a mesh axis runs over, the one named last changes fastest.
Arguments:
- tokens: bfloat16 [32, 1024, 1024], P('dp', 'ctx'), may hold values from -6 to 6
- segment_ids: int32 [32, 1024], P('dp', 'ctx'), may hold values from 0 to 3, as said below
- norm1_gain: bfloat16 [1024], P(('dp', 'ctx')), may hold values from 0.5 to 1.5
- norm1_shift: bfloat16 [1024], P(('dp', 'ctx')), may hold values from -1.75 to 1.75
- w_query: bfloat16 [1024, 1024], P(('dp', 'ctx'), 'tensor'), may hold values from -0.1875 to 0.1875
- w_key: bfloat16 [1024, 1024], P(('dp', 'ctx'), 'tensor'), may hold values from -0.1875 to 0.1875
- w_value: bfloat16 [1024, 1024], P(('dp', 'ctx'), 'tensor'), may hold values from -0.1875 to 0.1875
- query_bias: bfloat16 [16, 64], P('tensor', ('dp', 'ctx')), may hold values from -1.75 to 1.75
- value_bias: bfloat16 [16, 64], P('tensor', ('dp', 'ctx')), may hold values from -1.75 to 1.75
- w_out: bfloat16 [1024, 1024], P('tensor', ('dp', 'ctx')), may hold values from -0.75 to 0.75
- out_bias: bfloat16 [1024], P(('dp', 'ctx')), may hold values from -1.75 to 1.75
- norm2_gain: bfloat16 [1024], P(('dp', 'ctx')), may hold values from 0.5 to 1.5
- norm2_shift: bfloat16 [1024], P(('dp', 'ctx')), may hold values from -1.75 to 1.75
- w_up: bfloat16 [1024, 4096], P(('dp', 'ctx'), 'tensor'), may hold values from -0.1875 to 0.1875
- up_bias: bfloat16 [16, 256], P('tensor', ('dp', 'ctx')), may hold values from -1.75 to 1.75
- w_down: bfloat16 [4096, 1024], P('tensor', ('dp', 'ctx')), may hold values from -0.1875 to 0.1875
- down_bias: bfloat16 [1024], P(('dp', 'ctx')), may hold values from -1.75 to 1.75
- out_grad: bfloat16 [32, 1024, 1024], P('dp', 'ctx'), may hold values from -6 to 6
Outputs:
- outputs: bfloat16 [32, 1024, 1024], P('dp', 'ctx')
- tokens_grad: bfloat16 [32, 1024, 1024], P('dp', 'ctx')
- norm1_gain_grad: float32 [1024], P(('dp', 'ctx'))
- norm1_shift_grad: float32 [1024], P(('dp', 'ctx'))
- w_query_grad: float32 [1024, 1024], P(('dp', 'ctx'), 'tensor')
- w_key_grad: float32 [1024, 1024], P(('dp', 'ctx'), 'tensor')
- w_value_grad: float32 [1024, 1024], P(('dp', 'ctx'), 'tensor')
- query_bias_grad: float32 [16, 64], P('tensor', ('dp', 'ctx'))
- value_bias_grad: float32 [16, 64], P('tensor', ('dp', 'ctx'))
- w_out_grad: float32 [1024, 1024], P('tensor', ('dp', 'ctx'))
- out_bias_grad: float32 [1024], P(('dp', 'ctx'))
- norm2_gain_grad: float32 [1024], P(('dp', 'ctx'))
- norm2_shift_grad: float32 [1024], P(('dp', 'ctx'))
- w_up_grad: float32 [1024, 4096], P(('dp', 'ctx'), 'tensor')
- up_bias_grad: float32 [16, 256], P('tensor', ('dp', 'ctx'))
- w_down_grad: float32 [4096, 1024], P('tensor', ('dp', 'ctx'))
- down_bias_grad: float32 [1024], P(('dp', 'ctx'))
Inputs may be any that keep to these rules, and one draw needn't show every extreme that they name: `segment_ids`: ids start at 0 and never fall along a sequence. In each group of 16 sequences one (drawn) is a single document; every other sequence holds exactly four documents of 200 tokens or more each.
All inputs are finite; a program needn't handle non-finite values.
Results may differ from a plain program's by a relative error of at most 0.017.
Values may be sent and summed in bfloat16 or wider, within the bound.
A program may use at most 384 MiB of HBM per device.

v0:
```python
import math

import jax
import jax.numpy as jnp
from jax import lax
from jax.sharding import PartitionSpec as P

HEADS = 16
MICRO = 2
HEAD_DIM = 64


EPSILON = 1e-05


def layer_norm(values, gain, shift):
    centre = values - jnp.mean(values, axis=-1, keepdims=True)
    spread = jnp.mean(centre * centre, axis=-1, keepdims=True)
    return centre * lax.rsqrt(spread + EPSILON) * gain + shift


def gelu_tanh(values):
    return (
        0.5
        * values
        * (1.0 + jnp.tanh(0.7978845608028654 * (values + 0.044715 * values * values * values)))
    )


def matmul(left, right):
    return jnp.dot(left, right, preferred_element_type=jnp.float32)


def matmul_left(left, right):
    return lax.dot_general(
        left, right, (((0,), (0,)), ((), ())), preferred_element_type=jnp.float32
    )


def matmul_right(left, right):
    return lax.dot_general(
        left, right, (((1,), (1,)), ((), ())), preferred_element_type=jnp.float32
    )


def full_total(partial_value):
    return lax.psum(partial_value, "tensor")


def scores_of(query_heads, key_heads, query_seg, key_seg, slopes, query_first):
    query_count = query_heads.shape[1]
    key_count = key_heads.shape[1]
    head_width = query_heads.shape[3]
    raw_scores = jnp.einsum(
        "bqhd,bkhd->bhqk", query_heads, key_heads, preferred_element_type=jnp.float32
    )
    query_place = query_first + jnp.arange(query_count)
    key_place = jnp.arange(key_count)
    offsets = (key_place[None, :] - query_place[:, None]).astype(jnp.float32)
    scores = (
        raw_scores * (1.0 / math.sqrt(head_width))
        + slopes[None, :, None, None] * offsets[None, None]
    )
    causal = (key_place[None, :] <= query_place[:, None])[None, None]
    same_doc = query_seg[:, None, :, None] == key_seg[:, None, None, :]
    return jnp.where(causal & same_doc, scores, -1e30)


def shards(
    tokens,
    segment_ids,
    norm1_gain,
    norm1_shift,
    w_query,
    w_key,
    w_value,
    query_bias,
    value_bias,
    w_out,
    out_bias,
    norm2_gain,
    norm2_shift,
    w_up,
    up_bias,
    w_down,
    down_bias,
    out_grad,
):
    seqs_local, span_len, model_width = tokens.shape
    micro_seqs = seqs_local // MICRO
    row_count = micro_seqs * span_len
    heads_local = query_bias.shape[0]
    cols_local = heads_local * HEAD_DIM
    ff_local = w_up.shape[1]
    length_all = span_len * lax.axis_size("ctx")
    span_first = lax.axis_index("ctx") * span_len
    head_global = lax.axis_index("tensor") * heads_local + jnp.arange(heads_local)
    slopes = jnp.exp2(-8.0 * (head_global + 1).astype(jnp.float32) / HEADS)
    scale = 1.0 / math.sqrt(HEAD_DIM)
    grad_query = jnp.zeros((model_width, cols_local), jnp.float32)
    grad_key = jnp.zeros((model_width, cols_local), jnp.float32)
    grad_value = jnp.zeros((model_width, cols_local), jnp.float32)
    grad_qbias = jnp.zeros((heads_local, HEAD_DIM), jnp.float32)
    grad_vbias = jnp.zeros((heads_local, HEAD_DIM), jnp.float32)
    grad_wout = jnp.zeros((cols_local, model_width), jnp.float32)
    grad_small = jnp.zeros((6, model_width), jnp.float32)
    grad_up = jnp.zeros((model_width, ff_local), jnp.float32)
    grad_ubias = jnp.zeros((heads_local, ff_local // heads_local), jnp.float32)
    grad_down = jnp.zeros((ff_local, model_width), jnp.float32)
    outputs_list = []
    inputs_grad_list = []
    for micro_index in range(MICRO):
        first = micro_index * micro_seqs
        inputs = (
            tokens[first : first + micro_seqs].reshape(row_count, model_width).astype(jnp.float32)
        )
        query_seg = segment_ids[first : first + micro_seqs]
        cotangent = out_grad[first : first + micro_seqs].reshape(row_count, model_width)
        weights = (
            lax.all_gather(norm1_gain, ("dp", "ctx"), axis=0, tiled=True),
            lax.all_gather(norm1_shift, ("dp", "ctx"), axis=0, tiled=True),
            lax.all_gather(w_query, ("dp", "ctx"), axis=0, tiled=True),
            lax.all_gather(w_key, ("dp", "ctx"), axis=0, tiled=True),
            lax.all_gather(w_value, ("dp", "ctx"), axis=0, tiled=True),
            lax.all_gather(query_bias, ("dp", "ctx"), axis=1, tiled=True),
            lax.all_gather(value_bias, ("dp", "ctx"), axis=1, tiled=True),
            lax.all_gather(w_out, ("dp", "ctx"), axis=1, tiled=True),
            lax.all_gather(out_bias, ("dp", "ctx"), axis=0, tiled=True),
            lax.all_gather(norm2_gain, ("dp", "ctx"), axis=0, tiled=True),
            lax.all_gather(norm2_shift, ("dp", "ctx"), axis=0, tiled=True),
            lax.all_gather(w_up, ("dp", "ctx"), axis=0, tiled=True),
            lax.all_gather(up_bias, ("dp", "ctx"), axis=1, tiled=True),
            lax.all_gather(w_down, ("dp", "ctx"), axis=1, tiled=True),
            lax.all_gather(down_bias, ("dp", "ctx"), axis=0, tiled=True),
        )
        (
            gain_one,
            shift_one,
            full_query,
            full_key,
            full_value,
            bias_query,
            bias_value,
            full_out,
            bias_out,
            gain_two,
            shift_two,
            full_up,
            bias_up,
            full_down,
            bias_down,
        ) = weights
        gain_one = gain_one.astype(jnp.float32)
        shift_one = shift_one.astype(jnp.float32)
        gain_two = gain_two.astype(jnp.float32)
        shift_two = shift_two.astype(jnp.float32)
        bias_out = bias_out.astype(jnp.float32)
        bias_down = bias_down.astype(jnp.float32)
        normed_one = layer_norm(inputs, gain_one, shift_one).astype(jnp.bfloat16)
        queries = (
            matmul(normed_one, full_query) + bias_query.reshape(-1).astype(jnp.float32)
        ).astype(jnp.bfloat16)
        key_rows = matmul(normed_one, full_key).astype(jnp.bfloat16)
        value_rows = (
            matmul(normed_one, full_value) + bias_value.reshape(-1).astype(jnp.float32)
        ).astype(jnp.bfloat16)
        local_pairs = jnp.concatenate([key_rows, value_rows], axis=1).reshape(
            micro_seqs, span_len, 2 * cols_local
        )
        pairs_all, key_seg = (
            lax.all_gather(local_pairs, "ctx", axis=1, tiled=True),
            lax.all_gather(query_seg.astype(jnp.bfloat16), "ctx", axis=1, tiled=True),
        )
        key_seg = key_seg.astype(jnp.float32)
        query_segf = query_seg.astype(jnp.float32)
        key_heads = pairs_all[:, :, :cols_local].reshape(
            micro_seqs, length_all, heads_local, HEAD_DIM
        )
        value_heads = pairs_all[:, :, cols_local:].reshape(
            micro_seqs, length_all, heads_local, HEAD_DIM
        )
        query_heads = queries.reshape(micro_seqs, span_len, heads_local, HEAD_DIM)
        scores = scores_of(query_heads, key_heads, query_segf, key_seg, slopes, span_first)
        highest = jnp.max(scores, axis=-1, keepdims=True)
        exponent = jnp.exp(scores - highest)
        totals = jnp.sum(exponent, axis=-1, keepdims=True)
        softmaxed = exponent / totals
        log_total = highest + jnp.log(totals)
        mixed_heads = jnp.einsum(
            "bhqk,bkhd->bqhd",
            softmaxed.astype(jnp.bfloat16),
            value_heads,
            preferred_element_type=jnp.float32,
        )
        mixed_low = mixed_heads.reshape(row_count, cols_local).astype(jnp.bfloat16)
        attn_part = matmul(mixed_low, full_out)
        residual = inputs + full_total(attn_part) + bias_out
        normed_two = layer_norm(residual, gain_two, shift_two).astype(jnp.bfloat16)
        pre_act = matmul(normed_two, full_up) + bias_up.reshape(-1).astype(jnp.float32)
        activated = gelu_tanh(pre_act).astype(jnp.bfloat16)
        mlp_part = matmul(activated, full_down)
        result_rows = (residual + full_total(mlp_part) + bias_down).astype(jnp.bfloat16)
        outputs_list.append(result_rows.reshape(micro_seqs, span_len, model_width))
        weights_back = (
            lax.all_gather(norm1_gain, ("dp", "ctx"), axis=0, tiled=True),
            lax.all_gather(norm1_shift, ("dp", "ctx"), axis=0, tiled=True),
            lax.all_gather(w_query, ("dp", "ctx"), axis=0, tiled=True),
            lax.all_gather(w_key, ("dp", "ctx"), axis=0, tiled=True),
            lax.all_gather(w_value, ("dp", "ctx"), axis=0, tiled=True),
            lax.all_gather(query_bias, ("dp", "ctx"), axis=1, tiled=True),
            lax.all_gather(value_bias, ("dp", "ctx"), axis=1, tiled=True),
            lax.all_gather(w_out, ("dp", "ctx"), axis=1, tiled=True),
            lax.all_gather(out_bias, ("dp", "ctx"), axis=0, tiled=True),
            lax.all_gather(norm2_gain, ("dp", "ctx"), axis=0, tiled=True),
            lax.all_gather(norm2_shift, ("dp", "ctx"), axis=0, tiled=True),
            lax.all_gather(w_up, ("dp", "ctx"), axis=0, tiled=True),
            lax.all_gather(up_bias, ("dp", "ctx"), axis=1, tiled=True),
            lax.all_gather(w_down, ("dp", "ctx"), axis=1, tiled=True),
            lax.all_gather(down_bias, ("dp", "ctx"), axis=0, tiled=True),
        )
        back_query = weights_back[2]
        back_key = weights_back[3]
        back_value = weights_back[4]
        back_out = weights_back[7]
        back_up = weights_back[11]
        back_down = weights_back[13]
        gain_one = weights_back[0].astype(jnp.float32)
        shift_one = weights_back[1].astype(jnp.float32)
        gain_two = weights_back[9].astype(jnp.float32)
        shift_two = weights_back[10].astype(jnp.float32)
        act_grad = matmul_right(cotangent, back_down)
        unused, gelu_pull = jax.vjp(gelu_tanh, pre_act)
        pre_grad = gelu_pull(act_grad)[0].astype(jnp.bfloat16)
        grad_down = grad_down + matmul_left(activated, cotangent)
        grad_ubias = grad_ubias + jnp.sum(pre_grad.astype(jnp.float32), axis=0).reshape(
            heads_local, -1
        )
        grad_up = grad_up + matmul_left(normed_two, pre_grad)
        normed_two_back = matmul_right(pre_grad, back_up)
        unused, norm_pull = jax.vjp(layer_norm, residual, gain_two, shift_two)
        resid_grad, gain_two_grad, shift_two_grad = norm_pull(full_total(normed_two_back))
        cot_rows = cotangent.astype(jnp.float32)
        resid_grad = resid_grad + cot_rows
        attn_grad = resid_grad.astype(jnp.bfloat16)
        grad_wout = grad_wout + matmul_left(mixed_low, attn_grad)
        mixed_grad = matmul_right(attn_grad, back_out).astype(jnp.bfloat16)
        mixed_grad_heads = mixed_grad.reshape(micro_seqs, span_len, heads_local, HEAD_DIM)
        scores = scores_of(query_heads, key_heads, query_segf, key_seg, slopes, span_first)
        softmaxed = jnp.exp(scores - log_total)
        prob_grad = jnp.einsum(
            "bqhd,bkhd->bhqk", mixed_grad_heads, value_heads, preferred_element_type=jnp.float32
        )
        delta = jnp.sum(softmaxed * prob_grad, axis=-1, keepdims=True)
        score_grad = (softmaxed * (prob_grad - delta)).astype(jnp.bfloat16)
        query_grad = (
            jnp.einsum("bhqk,bkhd->bqhd", score_grad, key_heads, preferred_element_type=jnp.float32)
            * scale
        )
        query_low = query_grad.reshape(row_count, cols_local).astype(jnp.bfloat16)
        key_grad = (
            jnp.einsum(
                "bhqk,bqhd->bkhd", score_grad, query_heads, preferred_element_type=jnp.float32
            )
            * scale
        )
        value_grad = jnp.einsum(
            "bhqk,bqhd->bkhd",
            softmaxed.astype(jnp.bfloat16),
            mixed_grad_heads,
            preferred_element_type=jnp.float32,
        )
        pair_grad = jnp.concatenate(
            [
                key_grad.reshape(micro_seqs, length_all, cols_local),
                value_grad.reshape(micro_seqs, length_all, cols_local),
            ],
            axis=2,
        )
        pair_own = lax.psum_scatter(
            pair_grad.astype(jnp.bfloat16), "ctx", scatter_dimension=1, tiled=True
        ).astype(jnp.float32)
        key_low = pair_own[:, :, :cols_local].reshape(row_count, cols_local).astype(jnp.bfloat16)
        value_low = pair_own[:, :, cols_local:].reshape(row_count, cols_local).astype(jnp.bfloat16)
        grad_query = grad_query + matmul_left(normed_one, query_low)
        grad_key = grad_key + matmul_left(normed_one, key_low)
        grad_value = grad_value + matmul_left(normed_one, value_low)
        grad_qbias = grad_qbias + jnp.sum(query_low.astype(jnp.float32), axis=0).reshape(
            heads_local, HEAD_DIM
        )
        grad_vbias = grad_vbias + jnp.sum(value_low.astype(jnp.float32), axis=0).reshape(
            heads_local, HEAD_DIM
        )
        normed_one_back = (
            matmul_right(query_low, back_query)
            + matmul_right(key_low, back_key)
            + matmul_right(value_low, back_value)
        )
        unused, first_pull = jax.vjp(layer_norm, inputs, gain_one, shift_one)
        input_grad, gain_one_grad, shift_one_grad = first_pull(full_total(normed_one_back))
        input_grad = (input_grad + resid_grad).astype(jnp.bfloat16)
        inputs_grad_list.append(input_grad.reshape(micro_seqs, span_len, model_width))
        grad_small = grad_small + jnp.stack(
            [
                gain_one_grad,
                shift_one_grad,
                jnp.sum(resid_grad, axis=0),
                gain_two_grad,
                shift_two_grad,
                jnp.sum(cot_rows, axis=0),
            ],
            axis=0,
        )
    summed = (
        lax.psum_scatter(
            grad_query.astype(jnp.bfloat16), ("dp", "ctx"), scatter_dimension=0, tiled=True
        ).astype(jnp.float32),
        lax.psum_scatter(
            grad_key.astype(jnp.bfloat16), ("dp", "ctx"), scatter_dimension=0, tiled=True
        ).astype(jnp.float32),
        lax.psum_scatter(
            grad_value.astype(jnp.bfloat16), ("dp", "ctx"), scatter_dimension=0, tiled=True
        ).astype(jnp.float32),
        lax.psum_scatter(
            grad_qbias.astype(jnp.bfloat16), ("dp", "ctx"), scatter_dimension=1, tiled=True
        ).astype(jnp.float32),
        lax.psum_scatter(
            grad_vbias.astype(jnp.bfloat16), ("dp", "ctx"), scatter_dimension=1, tiled=True
        ).astype(jnp.float32),
        lax.psum_scatter(
            grad_wout.astype(jnp.bfloat16), ("dp", "ctx"), scatter_dimension=1, tiled=True
        ).astype(jnp.float32),
        lax.psum_scatter(
            grad_small.astype(jnp.bfloat16), ("dp", "ctx"), scatter_dimension=1, tiled=True
        ).astype(jnp.float32),
        lax.psum_scatter(
            grad_up.astype(jnp.bfloat16), ("dp", "ctx"), scatter_dimension=0, tiled=True
        ).astype(jnp.float32),
        lax.psum_scatter(
            grad_ubias.astype(jnp.bfloat16), ("dp", "ctx"), scatter_dimension=1, tiled=True
        ).astype(jnp.float32),
        lax.psum_scatter(
            grad_down.astype(jnp.bfloat16), ("dp", "ctx"), scatter_dimension=1, tiled=True
        ).astype(jnp.float32),
    )
    (
        sum_query,
        sum_key,
        sum_value,
        sum_qbias,
        sum_vbias,
        sum_wout,
        sum_small,
        sum_up,
        sum_ubias,
        sum_down,
    ) = summed
    return (
        jnp.concatenate(outputs_list, axis=0),
        jnp.concatenate(inputs_grad_list, axis=0),
        sum_small[0],
        sum_small[1],
        sum_query,
        sum_key,
        sum_value,
        sum_qbias,
        sum_vbias,
        sum_wout,
        sum_small[2],
        sum_small[3],
        sum_small[4],
        sum_up,
        sum_ubias,
        sum_down,
        sum_small[5],
    )


def solution(mesh):
    return jax.shard_map(
        shards,
        mesh=mesh,
        in_specs=(
            P("dp", "ctx", None),
            P("dp", "ctx"),
            P(("dp", "ctx")),
            P(("dp", "ctx")),
            P(("dp", "ctx"), "tensor"),
            P(("dp", "ctx"), "tensor"),
            P(("dp", "ctx"), "tensor"),
            P("tensor", ("dp", "ctx")),
            P("tensor", ("dp", "ctx")),
            P("tensor", ("dp", "ctx")),
            P(("dp", "ctx")),
            P(("dp", "ctx")),
            P(("dp", "ctx")),
            P(("dp", "ctx"), "tensor"),
            P("tensor", ("dp", "ctx")),
            P("tensor", ("dp", "ctx")),
            P(("dp", "ctx")),
            P("dp", "ctx", None),
        ),
        out_specs=(
            P("dp", "ctx", None),
            P("dp", "ctx", None),
            P(("dp", "ctx")),
            P(("dp", "ctx")),
            P(("dp", "ctx"), "tensor"),
            P(("dp", "ctx"), "tensor"),
            P(("dp", "ctx"), "tensor"),
            P("tensor", ("dp", "ctx")),
            P("tensor", ("dp", "ctx")),
            P("tensor", ("dp", "ctx")),
            P(("dp", "ctx")),
            P(("dp", "ctx")),
            P(("dp", "ctx")),
            P(("dp", "ctx"), "tensor"),
            P("tensor", ("dp", "ctx")),
            P("tensor", ("dp", "ctx")),
            P(("dp", "ctx")),
        ),
        check_vma=False,
    )
```

profile of v0, /device:TPU:0, one launch (start us, length us, event | category | flops | bytes accessed | tf_op | source)
XLA Modules:
  0.0 3331.2 jit_solution(2873348431085794174)
XLA Ops:
  17.0 10.2 all-gather
  27.3 8.7 all-gather.1
  36.0 8.9 all_gather.41
  44.9 8.9 all-gather.2
  54.0 8.9 all_gather.40
  62.9 7.5 fusion.48
  85.1 12.3 all_gather.45
  97.5 7.9 all-gather.3
  127.3 11.8 all_gather.47
  168.1 31.2 all-gather.20.cloned.1.call-done
  212.0 18.4 fusion.114
  230.4 14.1 fusion
  244.6 15.2 fusion.76
  259.8 18.3 fusion.113
  278.1 14.1 fusion.1
  292.3 15.4 fusion.77
  319.6 8.8 all-gather.4
  328.4 7.9 all-gather.5
  336.3 8.6 all-gather.6
  350.8 8.1 all-gather.7
  359.0 10.7 fusion.125
  369.8 512.8 %all-reduce.14.cloned.1.call-done = (f32[2048,1024]{1,0:T(8,128)}, f32[2048,1024]{1,0:T(8,128)}) async-done(((f32[2048,1024]{1,0:T(8,128)}, f32[2048,1024]{1,0:T(8,128)}), (f32[2048,1024]{1,0:T(8,128)}, f32[2048,1024]{1,0:T(8,128)})) %all-reduce.14.cloned.1.call-update) | async-done | bytes 16777232 | tf_op jit(solution)/shard_map/psum | solution.py:47
  882.5 13.1 fusion.106
  895.7 7.2 multiply_reduce_fusion.6
  911.2 10.9 fusion.118
  928.8 24.0 convert_reduce_fusion.3
  959.6 6.9 fusion.126
  967.4 562.6 %all-reduce.12.cloned.1.call-done = (f32[2048,1024]{1,0:T(8,128)}, f32[2048,1024]{1,0:T(8,128)}) async-done(((f32[2048,1024]{1,0:T(8,128)}, f32[2048,1024]{1,0:T(8,128)}), (f32[2048,1024]{1,0:T(8,128)}, f32[2048,1024]{1,0:T(8,128)})) %all-reduce.12.cloned.1.call-update) | async-done | bytes 16777232 | tf_op jit(solution)/shard_map/psum | solution.py:47
  1530.0 14.3 multiply_reduce_fusion.2
  1545.4 13.8 fusion.104
  1559.2 12.3 fusion.102
  1579.1 24.0 multiply_reduce_fusion
  1603.1 15.4 fusion.59
  1618.5 28.0 multiply_convert_fusion
  1646.5 10.8 multiply_convert_fusion.2
  1670.2 7.4 pad_maximum_fusion.2
  1689.0 25.1 multiply_reduce_fusion.1
  1714.1 28.6 multiply_convert_fusion.1
  1742.8 10.8 multiply_convert_fusion.3
  1760.0 15.4 fusion.56
  1781.9 7.4 pad_maximum_fusion.1
  1790.7 10.5 fusion.131
  1801.3 13.1 add_convert_fusion.6
  1817.6 10.3 fusion.37
  1838.8 9.1 fusion.119
  1847.9 12.5 fusion.99
  1864.1 10.1 convert_reduce_fusion.8
  1875.1 9.2 convert_reduce_fusion.9
  1930.9 10.5 add_add_fusion.4
  1941.4 10.6 add_add_fusion.5
  1952.7 8.8 all-gather.8
  1970.2 16.7 reduce-scatter.31.cloned.1.call-done
  1988.7 35.6 %reduce-scatter.35.cloned.1.call-done = bf16[128,256]{1,0:T(8,128)(2,1)} async-done(((bf16[1024,256]{1,0:T(8,128)(2,1)}), bf16[128,256]{1,0:T(8,128)(2,1)}) %reduce-scatter.35.cloned.1.call-update) | async-done | bytes 65552
  2026.0 35.6 %reduce-scatter.25.cloned.1.call-done = bf16[128,256]{1,0:T(8,128)(2,1)} async-done(((bf16[1024,256]{1,0:T(8,128)(2,1)}), bf16[128,256]{1,0:T(8,128)(2,1)}) %reduce-scatter.25.cloned.1.call-update) | async-done | bytes 65552 | tf_op jit(solution)/shard_map/reduce_scatter | solution.py:314
  2063.2 12.2 all-reduce.5
  2076.7 22.3 reduce-scatter.29.cloned.1.call-done
  2100.5 35.5 %reduce-scatter.27.cloned.1.call-done = bf16[128,256]{1,0:T(8,128)(2,1)} async-done(((bf16[1024,256]{1,0:T(8,128)(2,1)}), bf16[128,256]{1,0:T(8,128)(2,1)}) %reduce-scatter.27.cloned.1.call-update) | async-done | bytes 65552 | tf_op jit(solution)/shard_map/reduce_scatter | solution.py:317
  2137.5 1111.1 %all-reduce.10.cloned.1.call-done = (f32[2048,1024]{1,0:T(8,128)}, f32[2048,1024]{1,0:T(8,128)}, f32[2048,1024]{1,0:T(8,128)}, f32[2048,1024]{1,0:T(8,128)}) async-done(((f32[2048,1024]{1,0:T(8,128)}, f32[2048,1024]{1,0:T(8,128)}, f32[2048,1024]{1,0:T(8,128)}, f32[2048,1024]{1,0:T(8,128)}), (f32[2048,1024]{1,0:T(8,128)}, f32[2048,1024]{1,0:T(8,128)}, f32[2048,1024]{1,0:T(8,128)}, ...) | async-done | bytes 33554448 | tf_op jit(solution)/shard_map/psum | solution.py:47
  3248.7 10.2 fusion.54
  3261.7 10.0 fusion.49
  3272.9 18.5 add_convert_fusion.1
  3291.3 7.6 pad_maximum_fusion.3
  3298.9 16.6 add_convert_fusion.4
  3315.5 7.6 pad_maximum_fusion
  (409 shorter events, 263.8 us)
Async XLA Ops:
  7.2 20.1 copy-start.90
  7.2 28.8 copy-start.67
  7.2 37.7 %copy-start.86 = (bf16[4,8]{1,0:T(4,128)(2,1)S(1)}, bf16[4,8]{1,0:T(4,128)(2,1)}, u32[]{:S(2)}) copy-start(bf16[4,8]{1,0:T(4,128)(2,1)} %param.26) | copy-start | bytes 196
  7.2 148.1 %all-gather.14.cloned.1.call-start = ((), (), s32[]{:S(2)}) async-start(), calls=%async_computation.10 | async-start | bytes 10485760 | tf_op jit(solution)/shard_map/all_gather | solution.py:171
  7.3 46.7 %copy-start.68 = (bf16[128,256]{1,0:T(8,128)(2,1)S(1)}, bf16[128,256]{1,0:T(8,128)(2,1)}, u32[]{:S(2)}) copy-start(bf16[128,256]{1,0:T(8,128)(2,1)} %param.23) | copy-start | bytes 196612
  11.5 33.4 %copy-start.63 = (f32[8,256]{1,0:T(8,128)}, f32[8,256]{1,0:T(8,128)S(1)}, u32[]{:S(2)}) copy-start(f32[8,256]{1,0:T(8,128)S(1)} %get-tuple-element.97) | copy-start | bytes 24580
  11.6 33.4 %copy-start.65 = (f32[8,256]{1,0:T(8,128)}, f32[8,256]{1,0:T(8,128)S(1)}, u32[]{:S(2)}) copy-start(f32[8,256]{1,0:T(8,128)S(1)} %get-tuple-element.99) | copy-start | bytes 24580
  16.3 19.7 copy-start.59
  16.4 54.0 %copy-start.51 = (f32[2048]{0:T(1024)}, f32[2048]{0:T(1024)S(1)}, u32[]{:S(2)}) copy-start(f32[2048]{0:T(1024)S(1)} %rsqrt.50) | copy-start | bytes 24580
  17.0 19.0 copy-start.61
  17.0 53.4 %copy-start.53 = (f32[2048]{0:T(1024)}, f32[2048]{0:T(1024)S(1)}, u32[]{:S(2)}) copy-start(f32[2048]{0:T(1024)S(1)} %rsqrt.52) | copy-start | bytes 24580
  17.0 53.3 %copy-start.45 = (f32[1,2,8,128]{3,1,2,0:T(2,128)}, f32[1,2,8,128]{3,1,2,0:T(2,128)S(1)}, u32[]{:S(2)}) copy-start(f32[1,2,8,128]{3,1,2,0:T(2,128)S(1)} %copy.177) | copy-start | bytes 24580
  17.0 53.3 %copy-start.47 = (f32[1,2,8,128]{3,1,2,0:T(2,128)}, f32[1,2,8,128]{3,1,2,0:T(2,128)S(1)}, u32[]{:S(2)}) copy-start(f32[1,2,8,128]{3,1,2,0:T(2,128)S(1)} %copy.172) | copy-start | bytes 24580
  27.3 43.1 %copy-start.49 = (f32[8,1,128]{2,1,0:T(1,128)}, f32[8,1,128]{2,1,0:T(1,128)S(1)}, u32[]{:S(2)}) copy-start(f32[8,1,128]{2,1,0:T(1,128)S(1)} %convert_element_type.517) | copy-start | bytes 12292
  36.0 34.4 %copy-start.71 = (f32[8,1,128]{2,1,0:T(1,128)}, f32[8,1,128]{2,1,0:T(1,128)S(1)}, u32[]{:S(2)}) copy-start(f32[8,1,128]{2,1,0:T(1,128)S(1)} %convert_element_type.518) | copy-start | bytes 12292
  44.9 34.2 %copy-start.22 = (bf16[1024,256]{1,0:T(8,128)(2,1)}, bf16[1024,256]{1,0:T(8,128)(2,1)S(1)}, u32[]{:S(2)}) copy-start(bf16[1024,256]{1,0:T(8,128)(2,1)S(1)} %all_gather.41) | copy-start | bytes 1572868
  62.9 12.6 copy-start.24
  75.4 123.9 %all-gather.20.cloned.1.call-start = ((), (), s32[]{:S(2)}) async-start(), calls=%async_computation.13 | async-start | bytes 10485760 | tf_op jit(solution)/shard_map/all_gather | solution.py:171
  80.4 17.0 copy-start.87
  82.6 276.4 %all-gather.18.cloned.1.call-start = ((), (), s32[]{:S(2)}) async-start(), calls=%async_computation.12 | async-start | bytes 2359296 | tf_op jit(solution)/shard_map/all_gather | solution.py:133
  83.4 799.2 %all-reduce.14.cloned.1.call-start = ((), (), s32[]{:S(2)}) async-start(), calls=%async_computation.26 | async-start | bytes 33554432 | tf_op jit(solution)/shard_map/psum | solution.py:47
  97.5 15.0 copy-start.27
  110.2 17.2 copy-start.70
  116.8 95.1 %copy-start.12 = (bf16[8,256,4,64]{1,3,2,0:T(8,128)(2,1)}, bf16[8,256,4,64]{1,3,2,0:T(8,128)(2,1)S(1)}, u32[]{:S(2)}) copy-start(bf16[8,256,4,64]{1,3,2,0:T(8,128)(2,1)S(1)} %copy.122) | copy-start | bytes 3145732
  146.4 113.4 %copy-start.14 = (bf16[8,256,4,64]{1,3,2,0:T(8,128)(2,1)}, bf16[8,256,4,64]{1,3,2,0:T(8,128)(2,1)S(1)}, u32[]{:S(2)}) copy-start(bf16[8,256,4,64]{1,3,2,0:T(8,128)(2,1)S(1)} %copy.128) | copy-start | bytes 3145732
  230.4 14.2 copy-start.41
  244.5 15.2 copy-start.55
  278.1 14.2 copy-start.43
  292.2 15.4 copy-start.57
  318.9 17.3 copy-start.93
  319.0 592.2 %all-gather.16.cloned.1.call-start = ((), (), s32[]{:S(2)}) async-start(), calls=%async_computation.11 | async-start | bytes 2359296 | tf_op jit(solution)/shard_map/all_gather | solution.py:131
  319.6 1210.4 %all-reduce.12.cloned.1.call-start = ((), (), s32[]{:S(2)}) async-start(), calls=%async_computation.25 | async-start | bytes 33554432 | tf_op jit(solution)/shard_map/psum | solution.py:47
  359.0 569.8 %copy-start.82 = (f32[1,2,4,128]{3,1,2,0:T(2,128)}, f32[1,2,4,128]{3,1,2,0:T(2,128)S(1)}, u32[]{:S(2)}) copy-start(f32[1,2,4,128]{3,1,2,0:T(2,128)S(1)} %copy.176) | copy-start | bytes 12292
  966.6 934.3 %reduce-scatter.23.cloned.1.call-start = ((), (), s32[]{:S(2)}) async-start(), calls=%async_computation.15 | async-start | bytes 10485760 | tf_op jit(solution)/shard_map/reduce_scatter | solution.py:279
  1530.0 14.3 copy-start.6
  1530.0 15.4 copy-start.7
  1545.4 13.8 copy-start.8
  1618.5 28.0 copy-start.15
  1677.6 235.0 %reduce-scatter.21.cloned.1.call-start = ((), (), s32[]{:S(2)}) async-start(), calls=%async_computation.14 | async-start | bytes 10485760 | tf_op jit(solution)/shard_map/reduce_scatter | solution.py:279
  1714.1 28.6 copy-start.13
  1789.3 177.6 %reduce-scatter.37.cloned.1.call-start = ((), (), s32[]{:S(2)}) async-start(), calls=%async_computation.22 | async-start | bytes 73728
  1801.2 16.3 copy-start.50
  1801.2 16.3 copy-start.64
  1801.2 16.3 copy-start.66
  1801.3 16.3 copy-start.72
  1801.3 16.3 copy-start.73
  1801.3 16.3 copy-start.74
  1801.3 166.9 %reduce-scatter.39.cloned.1.call-start = ((), (), s32[]{:S(2)}) async-start(), calls=%async_computation.23 | async-start | bytes 2359296
  1817.0 169.9 %reduce-scatter.31.cloned.1.call-start = ((), (), s32[]{:S(2)}) async-start(), calls=%async_computation.19 | async-start | bytes 2359296 | tf_op jit(solution)/shard_map/reduce_scatter | solution.py:335
  1838.5 185.9 %reduce-scatter.35.cloned.1.call-start = ((), (), s32[]{:S(2)}) async-start(), calls=%async_computation.21 | async-start | bytes 589824
  1838.7 21.7 slice-start.2
  1838.8 23.0 slice-start.4
  1847.9 12.6 copy-start.17
  1847.9 13.9 slice-start.5
  1889.8 171.7 %reduce-scatter.25.cloned.1.call-start = ((), (), s32[]{:S(2)}) async-start(), calls=%async_computation.16 | async-start | bytes 589824 | tf_op jit(solution)/shard_map/reduce_scatter | solution.py:314
  1900.4 198.6 %reduce-scatter.29.cloned.1.call-start = ((), (), s32[]{:S(2)}) async-start(), calls=%async_computation.18 | async-start | bytes 589824 | tf_op jit(solution)/shard_map/reduce_scatter | solution.py:320
  1920.1 215.9 %reduce-scatter.27.cloned.1.call-start = ((), (), s32[]{:S(2)}) async-start(), calls=%async_computation.17 | async-start | bytes 589824 | tf_op jit(solution)/shard_map/reduce_scatter | solution.py:317
  1930.8 1317.9 %all-reduce.10.cloned.1.call-start = ((), (), s32[]{:S(2)}) async-start(), calls=%async_computation.24 | async-start | bytes 67108864 | tf_op jit(solution)/shard_map/psum | solution.py:47
  1952.0 1296.6 %copy-start.46 = (f32[1,2,8,128]{3,1,2,0:T(2,128)S(1)}, f32[1,2,8,128]{3,1,2,0:T(2,128)}, u32[]{:S(2)}) copy-start(f32[1,2,8,128]{3,1,2,0:T(2,128)} %copy-done.45) | copy-start | bytes 24580
  1952.1 1296.6 %copy-start.48 = (f32[1,2,8,128]{3,1,2,0:T(2,128)S(1)}, f32[1,2,8,128]{3,1,2,0:T(2,128)}, u32[]{:S(2)}) copy-start(f32[1,2,8,128]{3,1,2,0:T(2,128)} %copy-done.47) | copy-start | bytes 24580
  1952.1 1371.1 %reduce-scatter.33.cloned.1.call-start = ((), (), s32[]{:S(2)}) async-start(), calls=%async_computation.20 | async-start | bytes 294912
  3248.7 13.0 copy-start.4
  3248.7 13.0 copy-start.52
  3248.7 13.0 copy-start.54
  (64 other events, 382.5 us)
Sparse Core Ops, SparseCore 0:
  75.5 62.7 all-gather.13
  139.9 59.3 all-gather.19
  201.2 28.1 all-gather.17
  319.1 563.4 all-reduce.13
  884.3 26.8 all-gather.15
  966.7 563.2 all-reduce.11
  1677.8 70.7 reduce-scatter.22
  1789.4 71.3 reduce-scatter.20
  1864.3 33.2 reduce-scatter.36
  1901.1 41.2 reduce-scatter.38
  1945.7 41.1 reduce-scatter.30
  1990.2 34.1 reduce-scatter.34
  2027.4 34.0 reduce-scatter.24
  2064.8 34.1 reduce-scatter.28
  2101.9 34.0 reduce-scatter.26
  2139.6 1108.9 all-reduce.9
  3273.0 32.3 reduce-scatter.32
where the time goes:
time: 3340 us; the launch traced here: 3330 us
  waiting for transfers between devices  2370 us (71%)
  matrix products  405 us (12%)
  other arithmetic  291 us (9%)
  blocking collectives  142 us (4%)
  local copies, waits for them, and re-layouts  109 us (3%)
    psum x3, waiting for transfers between devices, full_total(): return lax.psum(partial_value, 'tensor')  2190 us
    dot_general x12, matrix products, matmul_right(): lax.dot_general(left, right, (((1,), (1,)), ((), ())), preferred_element_...  96.3 us
  transfers between devices with their start and end apart: 17, of which 10 were waited for; matrix products, arithmetic and copies ran while one was open for 16% of the time, Pallas kernels for 0%

commit v1 on v0

--- a/solution.py
+++ b/solution.py
@@ -1,8 +1,11 @@
+import functools
 import math
 
 import jax
 import jax.numpy as jnp
 from jax import lax
+from jax.experimental import pallas as pl
+from jax.experimental.pallas import tpu as pltpu
 from jax.sharding import PartitionSpec as P
 
 HEADS = 16
@@ -375,9 +378,347 @@
     )
 
 
+ALL = ("dp", "ctx", "tensor")
+NORMAL = (((1,), (0,)), ((), ()))
+ROWS = (((1,), (1,)), ((), ()))
+COLS = (((0,), (0,)), ((), ()))
+QUERY_BLOCK = 256
+
+
+def dot(left, right, dims):
+    return lax.dot_general(left, right, dims, preferred_element_type=jnp.float32)
+
+
+def scores_turned(query, key, slope, first, seg_query, seg_key, causal_from):
+    count, block = key.shape[0], query.shape[0]
+    raw = dot(key, query, ROWS) * (1.0 / math.sqrt(HEAD_DIM))
+    key_place = lax.broadcasted_iota(jnp.int32, (count, 1), 0)
+    query_place = first + lax.broadcasted_iota(jnp.int32, (1, block), 1)
+    scores = raw + slope * (key_place - query_place).astype(jnp.float32)
+    allowed = (key_place <= query_place) & (seg_key == seg_query)
+    return jnp.where(allowed, scores, -1e30)
+
+
+def attend_kernel(heads, block, slope_ref, row_ref, col_ref, qkv_ref, o_ref, lse_ref):
+    step = pl.program_id(1)
+    length = qkv_ref.shape[0]
+    width = heads * HEAD_DIM
+    for head in range(heads):
+        lo = head * HEAD_DIM
+        slope = slope_ref[step * heads + head]
+        for first in range(0, length, block):
+            last = first + block
+            query = qkv_ref[first:last, lo : lo + HEAD_DIM]
+            key = qkv_ref[0:last, width + lo : width + lo + HEAD_DIM]
+            value = qkv_ref[0:last, 2 * width + lo : 2 * width + lo + HEAD_DIM]
+            scores = scores_turned(
+                query, key, slope, first, row_ref[:, first:last], col_ref[0:last, :], first
+            )
+            highest = jnp.max(scores, axis=0, keepdims=True)
+            exponent = jnp.exp(scores - highest)
+            totals = jnp.sum(exponent, axis=0, keepdims=True)
+            softmaxed = (exponent * (1.0 / totals)).astype(jnp.bfloat16)
+            mixed = dot(softmaxed, value, COLS)
+            o_ref[first:last, lo : lo + HEAD_DIM] = mixed.astype(jnp.bfloat16)
+            lse_ref[head : head + 1, first:last] = highest + jnp.log(totals)
+
+
+def attend_back_kernel(
+    heads, block, slope_ref, row_ref, col_ref, qkv_ref, do_ref, lse_ref, grad_ref, dk_ref, dv_ref
+):
+    step = pl.program_id(1)
+    length = qkv_ref.shape[0]
+    width = heads * HEAD_DIM
+    scale = 1.0 / math.sqrt(HEAD_DIM)
+    for head in range(heads):
+        lo = head * HEAD_DIM
+        slope = slope_ref[step * heads + head]
+        for first in reversed(range(0, length, block)):
+            last = first + block
+            query = qkv_ref[first:last, lo : lo + HEAD_DIM]
+            key = qkv_ref[0:last, width + lo : width + lo + HEAD_DIM]
+            value = qkv_ref[0:last, 2 * width + lo : 2 * width + lo + HEAD_DIM]
+            mixed_grad = do_ref[first:last, lo : lo + HEAD_DIM]
+            scores = scores_turned(
+                query, key, slope, first, row_ref[:, first:last], col_ref[0:last, :], first
+            )
+            softmaxed = jnp.exp(scores - lse_ref[head : head + 1, first:last])
+            prob_grad = dot(value, mixed_grad, ROWS)
+            delta = jnp.sum(softmaxed * prob_grad, axis=0, keepdims=True)
+            score_grad = (softmaxed * (prob_grad - delta)).astype(jnp.bfloat16)
+            prob_low = softmaxed.astype(jnp.bfloat16)
+            query_grad = dot(score_grad, key, COLS) * scale
+            grad_ref[first:last, lo : lo + HEAD_DIM] = query_grad.astype(jnp.bfloat16)
+            key_grad = dot(score_grad, query, NORMAL)
+            value_grad = dot(prob_low, mixed_grad, NORMAL)
+            if last == length:
+                dk_ref[...] = key_grad
+                dv_ref[...] = value_grad
+            else:
+                dk_ref[0:last, :] += key_grad
+                dv_ref[0:last, :] += value_grad
+        grad_ref[:, width + lo : width + lo + HEAD_DIM] = (dk_ref[...] * scale).astype(jnp.bfloat16)
+        grad_ref[:, 2 * width + lo : 2 * width + lo + HEAD_DIM] = dv_ref[...].astype(jnp.bfloat16)
+
+
+def attention_specs(seqs, length, groups, heads):
+    width = heads * HEAD_DIM
+    return (
+        pl.BlockSpec(memory_space=pltpu.SMEM),
+        pl.BlockSpec((None, 1, length), lambda s, t: (s, 0, 0)),
+        pl.BlockSpec((None, length, 1), lambda s, t: (s, 0, 0)),
+        pl.BlockSpec((None, length, 3 * width), lambda s, t: (s, 0, t)),
+        pl.BlockSpec((None, length, width), lambda s, t: (s, 0, t)),
+        pl.BlockSpec((None, None, heads, length), lambda s, t: (s, t, 0, 0)),
+    )
+
+
+def attend(slopes, seg_row, seg_col, qkv, groups, heads):
+    seqs, length, _ = qkv.shape
+    specs = attention_specs(seqs, length, groups, heads)
+    block = math.gcd(length, QUERY_BLOCK)
+    return pl.pallas_call(
+        functools.partial(attend_kernel, heads, block),
+        grid=(seqs, groups),
+        in_specs=list(specs[:4]),
+        out_specs=[specs[4], specs[5]],
+        out_shape=[
+            jax.ShapeDtypeStruct((seqs, length, groups * heads * HEAD_DIM), jnp.bfloat16),
+            jax.ShapeDtypeStruct((seqs, groups, heads, length), jnp.float32),
+        ],
+        compiler_params=pltpu.CompilerParams(vmem_limit_bytes=40 * 2**20),
+        name="attend",
+    )(slopes, seg_row, seg_col, qkv)
+
+
+def attend_back(slopes, seg_row, seg_col, qkv, mixed_grad, log_total, groups, heads):
+    seqs, length, _ = qkv.shape
+    specs = attention_specs(seqs, length, groups, heads)
+    block = math.gcd(length, QUERY_BLOCK)
+    return pl.pallas_call(
+        functools.partial(attend_back_kernel, heads, block),
+        grid=(seqs, groups),
+        in_specs=list(specs),
+        out_specs=specs[3],
+        out_shape=jax.ShapeDtypeStruct(qkv.shape, jnp.bfloat16),
+        scratch_shapes=[
+            pltpu.VMEM((length, HEAD_DIM), jnp.float32),
+            pltpu.VMEM((length, HEAD_DIM), jnp.float32),
+        ],
+        compiler_params=pltpu.CompilerParams(vmem_limit_bytes=40 * 2**20),
+        name="attend_back",
+    )(slopes, seg_row, seg_col, qkv, mixed_grad, log_total)
+
+
+def whole_sequences(
+    tokens,
+    segment_ids,
+    norm1_gain,
+    norm1_shift,
+    w_query,
+    w_key,
+    w_value,
+    query_bias,
+    value_bias,
+    w_out,
+    out_bias,
+    norm2_gain,
+    norm2_shift,
+    w_up,
+    up_bias,
+    w_down,
+    down_bias,
+    out_grad,
+):
+    dps, ctxs, groups = (lax.axis_size(name) for name in ALL)
+    owners = dps * ctxs
+    place = lax.axis_index("tensor")
+    seqs_local, span, model = tokens.shape
+    per_group = seqs_local // groups
+    seqs = per_group // ctxs
+    length = span * ctxs
+    rows = seqs * length
+    heads = query_bias.shape[0]
+    width = heads * HEAD_DIM
+    shard = w_query.shape[0]
+    hidden = w_up.shape[1]
+    shared = query_bias.shape[1]
+    shared_up = up_bias.shape[1]
+
+    def gather(value):
+        whole = lax.all_gather(value, ALL, axis=0, tiled=False)
+        return whole.reshape((owners, groups) + value.shape)
+
+    def to_sequences(value):
+        mine = lax.dynamic_slice_in_dim(value, place * per_group, per_group, axis=0)
+        return lax.all_to_all(mine, "ctx", split_axis=0, concat_axis=1, tiled=True)
+
+    def to_spans(value):
+        mine = lax.all_to_all(value, "ctx", split_axis=1, concat_axis=0, tiled=True)
+        return lax.all_gather(mine, "tensor", axis=0, tiled=True)
+
+    def scatter(value):
+        return lax.psum_scatter(value, ALL, scatter_dimension=0, tiled=True)
+
+    small = jnp.concatenate(
+        [
+            norm1_gain,
+            norm1_shift,
+            out_bias,
+            norm2_gain,
+            norm2_shift,
+            down_bias,
+            query_bias.reshape(-1),
+            value_bias.reshape(-1),
+            up_bias.reshape(-1),
+        ]
+    )
+    small = gather(small)
+    vectors = small[:, 0, : 6 * shard].reshape(owners, 6, shard).transpose(1, 0, 2)
+    vectors = vectors.reshape(6, model).astype(jnp.float32)
+    gain_one, shift_one, bias_out, gain_two, shift_two, bias_down = (
+        vectors[index] for index in range(6)
+    )
+
+    def heads_bias(first, columns):
+        part = small[:, :, first : first + heads * columns]
+        part = part.reshape(owners, groups, heads, columns).transpose(1, 2, 0, 3)
+        return part.reshape(groups, heads * columns * owners).astype(jnp.float32)
+
+    bias_first = 6 * shard
+    bias_query = heads_bias(bias_first, shared)
+    bias_value = heads_bias(bias_first + heads * shared, shared)
+    bias_up = heads_bias(bias_first + 2 * heads * shared, shared_up).reshape(-1)
+    bias_qkv = jnp.stack([bias_query, jnp.zeros_like(bias_query), bias_value], axis=1).reshape(-1)
+
+    full_qkv = gather(jnp.concatenate([w_query, w_key, w_value], axis=1))
+    full_qkv = full_qkv.transpose(0, 2, 1, 3).reshape(model, groups * 3 * width)
+    full_out = gather(w_out).transpose(1, 2, 0, 3).reshape(groups * width, model)
+    full_up = gather(w_up).transpose(0, 2, 1, 3).reshape(model, groups * hidden)
+    full_down = gather(w_down).transpose(1, 2, 0, 3).reshape(groups * hidden, model)
+
+    inputs_low = to_sequences(tokens)
+    segs = to_sequences(segment_ids)
+    cotangent = to_sequences(out_grad).reshape(rows, model)
+    seg_row = segs.reshape(seqs, 1, length)
+    seg_col = segs.reshape(seqs, length, 1)
+    slopes = jnp.exp2(-8.0 * jnp.arange(1, HEADS + 1).astype(jnp.float32) / HEADS)
+
+    inputs = inputs_low.reshape(rows, model).astype(jnp.float32)
+    normed_one = layer_norm(inputs, gain_one, shift_one).astype(jnp.bfloat16)
+    qkv = (matmul(normed_one, full_qkv) + bias_qkv).astype(jnp.bfloat16)
+    qkv = qkv.reshape(seqs, length, groups * 3 * width)
+    mixed, log_total = attend(slopes, seg_row, seg_col, qkv, groups, heads)
+    mixed = mixed.reshape(rows, groups * width)
+    residual = inputs + matmul(mixed, full_out) + bias_out
+    normed_two = layer_norm(residual, gain_two, shift_two).astype(jnp.bfloat16)
+    pre_act = matmul(normed_two, full_up) + bias_up
+    activated = gelu_tanh(pre_act).astype(jnp.bfloat16)
+    result = (residual + matmul(activated, full_down) + bias_down).astype(jnp.bfloat16)
+    outputs = to_spans(result.reshape(seqs, length, model))
+
+    act_grad = matmul_right(cotangent, full_down)
+    unused, gelu_pull = jax.vjp(gelu_tanh, pre_act)
+    pre_grad = gelu_pull(act_grad)[0].astype(jnp.bfloat16)
+    grad_down = matmul_left(activated, cotangent)
+    grad_down = grad_down.reshape(groups, hidden, owners, shard).transpose(2, 0, 1, 3)
+    sum_down = scatter(grad_down.astype(jnp.bfloat16).reshape(-1, shard)).astype(jnp.float32)
+    grad_ubias = jnp.sum(pre_grad.astype(jnp.float32), axis=0)
+    grad_up = matmul_left(normed_two, pre_grad)
+    grad_up = grad_up.reshape(owners, shard, groups, hidden).transpose(0, 2, 1, 3)
+    sum_up = scatter(grad_up.astype(jnp.bfloat16).reshape(-1, hidden)).astype(jnp.float32)
+    normed_two_back = matmul_right(pre_grad, full_up)
+    unused, norm_pull = jax.vjp(layer_norm, residual, gain_two, shift_two)
+    resid_grad, gain_two_grad, shift_two_grad = norm_pull(normed_two_back)
+    cot_rows = cotangent.astype(jnp.float32)
+    resid_grad = resid_grad + cot_rows
+    attn_grad = resid_grad.astype(jnp.bfloat16)
+    mixed_grad = matmul_right(attn_grad, full_out).astype(jnp.bfloat16)
+    grad_wout = matmul_left(mixed, attn_grad)
+    grad_wout = grad_wout.reshape(groups, width, owners, shard).transpose(2, 0, 1, 3)
+    sum_wout = scatter(grad_wout.astype(jnp.bfloat16).reshape(-1, shard)).astype(jnp.float32)
+    qkv_grad = attend_back(
+        slopes,
+        seg_row,
+        seg_col,
+        qkv,
+        mixed_grad.reshape(seqs, length, groups * width),
+        log_total,
+        groups,
+        heads,
+    ).reshape(rows, groups * 3 * width)
+    normed_one_back = matmul_right(qkv_grad, full_qkv)
+    unused, first_pull = jax.vjp(layer_norm, inputs, gain_one, shift_one)
+    input_grad, gain_one_grad, shift_one_grad = first_pull(normed_one_back)
+    input_grad = (input_grad + resid_grad).astype(jnp.bfloat16)
+    tokens_grad = to_spans(input_grad.reshape(seqs, length, model))
+    grad_qkv = matmul_left(normed_one, qkv_grad)
+    grad_qkv = grad_qkv.reshape(owners, shard, groups, 3 * width).transpose(0, 2, 1, 3)
+    sum_qkv = scatter(grad_qkv.astype(jnp.bfloat16).reshape(-1, 3 * width)).astype(jnp.float32)
+    grad_bias = jnp.sum(qkv_grad.astype(jnp.float32), axis=0).reshape(groups, 3, heads, HEAD_DIM)
+
+    grad_vectors = jnp.stack(
+        [
+            gain_one_grad,
+            shift_one_grad,
+            jnp.sum(resid_grad, axis=0),
+            gain_two_grad,
+            shift_two_grad,
+            jnp.sum(cot_rows, axis=0),
+        ]
+    )
+    grad_vectors = grad_vectors.reshape(6, owners, shard).transpose(1, 0, 2)
+    grad_vectors = jnp.broadcast_to(
+        grad_vectors.reshape(owners, 1, 6 * shard), (owners, groups, 6 * shard)
+    )
+
+    def owner_bias(value, columns):
+        value = value.reshape(groups, heads, owners, columns).transpose(2, 0, 1, 3)
+        return value.reshape(owners, groups, heads * columns)
+
+    grad_small = jnp.concatenate(
+        [
+            grad_vectors,
+            owner_bias(grad_bias[:, 0], shared),
+            owner_bias(grad_bias[:, 2], shared),
+            owner_bias(grad_ubias, shared_up),
+        ],
+        axis=2,
+    )
+    sum_small = scatter(grad_small.reshape(owners * groups, -1))[0]
+    sums = sum_small[: 6 * shard].reshape(6, shard)
+    sum_biases = sum_small[6 * shard :]
+    count = heads * shared
+    return (
+        outputs,
+        tokens_grad,
+        sums[0],
+        sums[1],
+        sum_qkv[:, :width],
+        sum_qkv[:, width : 2 * width],
+        sum_qkv[:, 2 * width :],
+        sum_biases[:count].reshape(heads, shared),
+        sum_biases[count : 2 * count].reshape(heads, shared),
+        sum_wout,
+        sums[2],
+        sums[3],
+        sums[4],
+        sum_up,
+        sum_biases[2 * count :].reshape(heads, shared_up),
+        sum_down,
+        sums[5],
+    )
+
+
+def choose_plan(tokens, *others):
+    if tokens.shape[0] % (lax.axis_size("ctx") * lax.axis_size("tensor")) == 0:
+        return whole_sequences(tokens, *others)
+    return shards(tokens, *others)
+
+
 def solution(mesh):
     return jax.shard_map(
-        shards,
+        choose_plan,
         mesh=mesh,
         in_specs=(
             P("dp", "ctx", None),

time: 3340 us -> 1560 us (0.47)
  waiting for transfers between devices: 2370 us -> 898 us
  matrix products: 405 us -> 155 us
  other arithmetic: 291 us -> 59.2 us
  local copies, waits for them, and re-layouts: 109 us -> 200 us
  Pallas kernels: 0 us -> 83.9 us
    psum x3 -> x0, waiting for transfers between devices: 2190 us -> none  [full_total(): return lax.psum(partial_value, 'tensor')]
    reduce_scatter x6 -> x4, waiting for transfers between devices: 110 us -> 488 us  [scatter(): return lax.psum_scatter(value, ALL, scatter_dimension=0, tiled=True)]
    all_gather x4 -> x6, waiting for transfers between devices: 32 us -> 382 us  [the longest x2 298 us: to_spans(): return lax.all_gather(mine, 'tensor', axis=0, tiled=True)]
    dot_general x12 -> x0, matrix products: 188 us -> none  [the longest x2 49.1 us: shards(): jnp.einsum('bqhd,bkhd->bhqk', mixed_grad_heads, value_heads, preferred_el...]
    all_gather x15 -> x0, blocking collectives: 130 us -> none  [the longest x1 12.3 us: shards(): lax.all_gather(w_query, ('dp', 'ctx'), axis=0, tiled=True)]
    convert_element_type x34 -> x8, other arithmetic: 125 us -> 8.28 us  [the longest x1 2.14 us: whole_sequences(): normed_one = layer_norm(inputs, gain_one, shift_one).astype(jnp.bfloat16)]
    pallas_call x0 -> x2, Pallas kernels: none -> 83.9 us  [the longest x1 50.1 us: attend_back(): pl.pallas_call(functools.partial(attend_back_kernel, heads, block), grid=...]
    all_to_all x0 -> x2, blocking collectives: none -> 63.1 us  [to_spans(): mine = lax.all_to_all(value, 'ctx', split_axis=1, concat_axis=0, tiled=True)]
  transfers between devices with their start and end apart: 17 -> 14, of which waited for: 10 -> 10; matrix products, arithmetic and copies ran while one was open for 16% -> 18% of each run, Pallas kernels for 0% -> 2%
where the time goes in v1:
time: 1560 us; the launch traced here: 1550 us
  waiting for transfers between devices  898 us (58%)
  local copies, waits for them, and re-layouts  200 us (13%)
  matrix products  155 us (10%)
  blocking collectives  124 us (8%)
  Pallas kernels  83.9 us (5%)
  other arithmetic  59.2 us (4%)
    reduce_scatter x4, waiting for transfers between devices, scatter(): return lax.psum_scatter(value, ALL, scatter_dimension=0, tiled=True)  488 us
    all_gather x2, waiting for transfers between devices, to_spans(): return lax.all_gather(mine, 'tensor', axis=0, tiled=True)  298 us
    all_gather x4, waiting for transfers between devices, gather(): whole = lax.all_gather(value, ALL, axis=0, tiled=False)  83.4 us
    all_to_all x2, blocking collectives, to_spans(): mine = lax.all_to_all(value, 'ctx', split_axis=1, concat_axis=0, tiled=True)  63.1 us
    unnamed x1, blocking collectives  61.4 us
    dot_general x4, matrix products, matmul_right(): lax.dot_general(left, right, (((1,), (1,)), ((), ())), preferred_element_...  56.2 us
    unnamed x86, local copies, waits for them, and re-layouts  55.5 us
    dot_general x4, matrix products, matmul(): return jnp.dot(left, right, preferred_element_type=jnp.float32)  54.8 us
  transfers between devices with their start and end apart: 14, of which 10 were waited for; matrix products, arithmetic and copies ran while one was open for 18% of the time, Pallas kernels for 2%

profile of v1, /device:TPU:0, one launch (start us, length us, event | category | flops | bytes accessed | tf_op | source)
XLA Modules:
  0.0 1548.1 jit_solution(13060629015596570074)
XLA Ops:
  11.6 4.2 all-to-all-start.1
  15.9 3.1 constant_dynamic-slice_fusion.2
  19.6 3.6 all-to-all-start
  23.9 61.4 %all-reduce = bf16[30720]{0:T(1024)(128)(2,1)S(1)} all-reduce(bf16[30720]{0:T(1024)(128)(2,1)S(1)} %dynamic-update-slice), channel_id=2, replica_groups=mesh['dp'=2,'ctx'=4,'tensor'=4] {'dp','ctx','tensor'}, use_global_device_ids=true, to_apply=%add | all-reduce | flops 30720 | bytes 122880
  86.0 3.1 constant_dynamic-slice_fusion
  89.2 4.5 all-to-all-start.3
  97.1 26.1 %all-to-all-done.3 = bf16[4,256,1024]{2,1,0:T(8,128)(2,1)} async-done(((bf16[4,256,1024]{2,1,0:T(8,128)(2,1)}), bf16[4,256,1024]{2,1,0:T(8,128)(2,1)}, u32[]{:S(2)}, u32[]{:S(2)}) %all-to-all-start.3) | async-done | bytes 2097184 | tf_op jit(solution)/shard_map/all_to_all | solution.py:554
  123.2 3.9 copy.182
  127.1 3.0 copy.181
  130.1 2.5 convert_reduce_fusion.2
  132.7 2.1 add_convert_fusion.5
  134.8 4.3 copy.157
  139.1 4.5 all-gather.16.cloned.1.call-done
  143.6 9.2 copy.152
  152.9 9.9 fusion.25.qkv_ref
  162.8 33.8 %attend.1 = (bf16[1,1024,1024]{2,1,0:T(8,128)(2,1)S(1)}, f32[1,4,4,1024]{3,2,1,0:T(4,128)S(1)}) custom-call(f32[16]{0:T(128)S(1)} %multiply_exponential_fusion.slope_ref, s32[1,1,1024]{2,1,0:T(1,128)S(1)} %bitcast.230, s32[1,1024,1]{2,1,0:T(8,128)S(1)} %copy.156.col_ref, bf16[1,1024,3072]{2,1,0:T(8,128)(2,1)S(1)} %fusion.25.qkv_ref), custom_call_target="tpu_custom_call" | custom-call | tf_op jit(solution)/shard_map/attend/pallas_call | solution.py:480
  196.6 2.6 copy-done.3
  199.1 2.6 copy.184
  201.7 5.6 fusion.68
  207.3 1.9 copy-done.9
  209.7 13.0 all-gather.20.cloned.1.call-done
  222.7 12.8 copy.158
  235.6 65.9 %all-gather.22.cloned.1.call-done = bf16[32768,128]{1,0:T(8,128)(2,1)} async-done(((bf16[1024,128]{1,0:T(8,128)(2,1)}), bf16[32768,128]{1,0:T(8,128)(2,1)}) %all-gather.22.cloned.1.call-update) | async-done | bytes 8388624 | tf_op jit(solution)/shard_map/all_gather | solution.py:549
  301.4 12.2 copy.160
  313.6 22.4 %fusion.10 = (bf16[4096,1024]{0,1:T(8,128)(2,1)}, f32[1024,4096]{1,0:T(8,128)}) fusion(f32[4096]{0:T(1024)S(1)} %reshape.423, bf16[512,8,8,128]{3,2,1,0:T(8,128)(2,1)} %bitcast.247, f32[1024,1024]{0,1:T(8,128)} %copy-done.9, f32[1024]{0:T(1024)S(1)} %get-tuple-element.49, f32[1024]{0:T(1024)S(1)} %get-tuple-element.47, f32[1024]{0:T(1024)S(1)} %fusion.56, ...), kind=kOutput, calls=%fused_computation.15 | convolution fusion | flops 8637120512 | bytes 37781504 | tf_op jit(solution)/shard_map/dot_general | solution.py:34
  336.0 28.7 %convert_reduce_fusion = (f32[4096]{0:T(1024)S(1)}, bf16[1024,4096]{1,0:T(8,128)(2,1)}) fusion(bf16[1024,1024]{1,0:T(8,128)(2,1)} %bitcast.27, bf16[512,8,8,128]{3,2,1,0:T(8,128)(2,1)} %bitcast.245, f32[1024,4096]{1,0:T(8,128)} %get-tuple-element.67, f32[4096]{0:T(1024)S(1)} %reshape.423), kind=kOutput, calls=%fused_computation.17 | convolution fusion | flops 8703176704 | bytes 35684352 | tf_op jit(solution)/shard_map/dot_general | solution.py:44
  364.7 16.6 %multiply_reduce_fusion = (f32[1024]{0:T(1024)S(1)}, f32[1024]{0:T(1024)S(1)}, f32[1024]{0:T(1024)S(1)}, f32[1024,1024]{0,1:T(8,128)}) fusion(f32[1024,1024]{0,1:T(8,128)} %copy-done.9, f32[1024]{0:T(1024)S(1)} %fusion.56, f32[1024]{0:T(1024)S(1)} %broadcast_multiply_fusion, f32[1024]{0:T(1024)S(1)} %get-tuple-element.47, ...), kind=kOutput, calls=%fused_computation.47 | convolution fusion | flops 8598320128 | bytes 25190400 | tf_op jit(solution)/shard_map/dot_general | solution.py:44
  381.3 4.7 fusion.65
  389.1 2.4 convert_bitcast_fusion.2.do_ref
  391.5 50.1 %attend_back.1 = bf16[1,1024,3072]{2,1,0:T(8,128)(2,1)S(1)} custom-call(f32[16]{0:T(128)S(1)} %multiply_exponential_fusion.slope_ref, s32[1,1,1024]{2,1,0:T(1,128)S(1)} %bitcast.231, s32[1,1024,1]{2,1,0:T(8,128)S(1)} %copy.156.col_ref, bf16[1,1024,3072]{2,1,0:T(8,128)(2,1)} %copy-done.3, bf16[1,1024,1024]{2,1,0:T(8,128)(2,1)S(1)} %convert_bitcast_fusion.2.do_ref, ...), custom_call_target="tpu_custom_call" | custom-call | tf_op jit(solution)/shard_map/attend_back/pallas_call | solution.py:498
  441.7 8.5 fusion.69
  451.8 5.4 copy.165
  457.3 4.2 multiply_reduce_fusion.2
  463.2 2.1 multiply_reduce_fusion.1
  465.4 4.2 fusion.54
  470.6 4.6 convert_bitcast_fusion.1
  476.8 8.8 copy.183
  485.6 11.1 convolution_convert_fusion.1
  497.4 17.0 %fusion.51 = bf16[1,1024,1024]{1,2,0:T(8,128)(2,1)} fusion(f32[1024]{0:T(1024)S(1)} %copy-done.22, f32[1024,1024]{0,1:T(8,128)} %copy-done.9, bf16[512,8,8,128]{3,2,1,0:T(8,128)(2,1)} %bitcast.246, f32[1024,4096]{1,0:T(8,128)} %get-tuple-element.67, f32[4096]{0:T(1024)S(1)} %reshape.423), kind=kOutput, calls=%fused_computation.71 | convolution fusion | flops 8635023360 | bytes 31477760 | tf_op jit(solution)/shard_map/dot_general | solution.py:34
  514.4 10.7 copy.162
  525.6 14.1 reduce.21
  539.7 4.5 reshape.464
  544.2 30.8 %all_to_all.55 = bf16[4,2,131072]{2,1,0:T(2,128)(2,1)} all-to-all(bf16[4,2,131072]{2,1,0:T(2,128)(2,1)} %reshape.464), channel_id=1, replica_groups=mesh['dp'=2,'ctx'=4,'tensor'=4] {'ctx'}, dimensions={0} | all-to-all | bytes 4194304 | tf_op jit(solution)/shard_map/all_to_all | solution.py:557
  575.0 4.9 reshape.465
  580.0 4.3 copy.186
  584.4 10.7 copy.166
  595.1 14.1 reduce.22
  609.2 4.5 reshape.466
  613.7 32.3 %all_to_all.56 = bf16[4,2,131072]{2,1,0:T(2,128)(2,1)} all-to-all(bf16[4,2,131072]{2,1,0:T(2,128)(2,1)} %reshape.466), channel_id=1, replica_groups=mesh['dp'=2,'ctx'=4,'tensor'=4] {'ctx'}, dimensions={0} | all-to-all | bytes 4194304 | tf_op jit(solution)/shard_map/all_to_all | solution.py:557
  646.0 4.9 reshape.467
  650.9 4.4 copy.187
  655.4 12.0 copy.185
  667.3 12.5 convert_bitcast_fusion
  679.8 7.5 copy.176
  688.0 15.6 %convolution_convert_fusion = bf16[1024,4096]{1,0:T(8,128)(2,1)} fusion(bf16[1024,4096]{1,0:T(8,128)(2,1)} %get-tuple-element.63, f32[1024,1024]{0,1:T(8,128)} %copy-done.9, f32[1024]{0:T(1024)S(1)} %copy-done.21, f32[1024]{0:T(1024)S(1)} %get-tuple-element.47, f32[1024]{0:T(1024)S(1)} %fusion.56, f32[1024]{0:T(1024)S(1)} %broadcast_multiply_fusion), kind=kOutput, calls=%fused_computation.30 | convolution fusion | flops 8599371776 | bytes 20987904 | tf_op jit(solution)/shard_map/dot_general | solution.py:38
  703.6 14.5 convert_element_type.209
  718.1 10.0 copy.174
  733.9 116.9 %reduce-scatter.5.cloned.1.call-done = bf16[128,768]{1,0:T(8,128)(2,1)} async-done(((bf16[4096,768]{1,0:T(8,128)(2,1)}), bf16[128,768]{1,0:T(8,128)(2,1)}) %reduce-scatter.5.cloned.1.call-update) | async-done | bytes 196624 | tf_op jit(solution)/shard_map/reduce_scatter | solution.py:561
  852.5 148.8 %all-gather.12.cloned.1.call-done = bf16[16,256,1024]{2,1,0:T(8,128)(2,1)} async-done(((bf16[4,256,1024]{2,1,0:T(8,128)(2,1)}), bf16[16,256,1024]{2,1,0:T(8,128)(2,1)}) %all-gather.12.cloned.1.call-update) | async-done | bytes 8388624 | tf_op jit(solution)/shard_map/all_gather | solution.py:558
  1001.2 149.5 %all-gather.14.cloned.1.call-done = bf16[16,256,1024]{2,1,0:T(8,128)(2,1)} async-done(((bf16[4,256,1024]{2,1,0:T(8,128)(2,1)}), bf16[16,256,1024]{2,1,0:T(8,128)(2,1)}) %all-gather.14.cloned.1.call-update) | async-done | bytes 8388624 | tf_op jit(solution)/shard_map/all_gather | solution.py:558
  1150.7 186.2 %reduce-scatter.11.cloned.1.call-done = bf16[1024,128]{1,0:T(8,128)(2,1)} async-done(((bf16[32768,128]{1,0:T(8,128)(2,1)}), bf16[1024,128]{1,0:T(8,128)(2,1)}) %reduce-scatter.11.cloned.1.call-update) | async-done | bytes 262160 | tf_op jit(solution)/shard_map/reduce_scatter | solution.py:561
  1338.7 184.6 %reduce-scatter.9.cloned.1.call-done = bf16[128,1024]{1,0:T(8,128)(2,1)} async-done(((bf16[4096,1024]{1,0:T(8,128)(2,1)}), bf16[128,1024]{1,0:T(8,128)(2,1)}) %reduce-scatter.9.cloned.1.call-update) | async-done | bytes 262160 | tf_op jit(solution)/shard_map/reduce_scatter | solution.py:561
  1525.1 8.1 copy.265
  1533.2 8.1 copy.266
  (170 shorter events, 32.1 us)
Async XLA Ops:
  7.2 3.7 copy-start
  7.2 127.6 %all-gather.18.cloned.1.call-start = ((), (), s32[]{:S(2)}) async-start(), calls=%async_computation.16 | async-start | bytes 2162688 | tf_op jit(solution)/shard_map/all_gather | solution.py:549
  7.9 135.7 %all-gather.16.cloned.1.call-start = ((), (), s32[]{:S(2)}) async-start(), calls=%async_computation.15 | async-start | bytes 6488064 | tf_op jit(solution)/shard_map/all_gather | solution.py:549
  9.6 213.1 %all-gather.20.cloned.1.call-start = ((), (), s32[]{:S(2)}) async-start(), calls=%async_computation.17 | async-start | bytes 8650752 | tf_op jit(solution)/shard_map/all_gather | solution.py:549
  10.3 291.1 %all-gather.22.cloned.1.call-start = ((), (), s32[]{:S(2)}) async-start(), calls=%async_computation.18 | async-start | bytes 8650752 | tf_op jit(solution)/shard_map/all_gather | solution.py:549
  11.6 8.0 all-to-all-start.1
  15.8 7.4 copy-start.29
  15.8 7.5 copy-start.30
  15.8 7.6 copy-start.31
  15.8 7.7 copy-start.23
  15.8 7.7 copy-start.24
  15.8 7.7 copy-start.25
  15.8 7.7 copy-start.26
  15.9 7.7 copy-start.27
  15.9 7.7 copy-start.28
  19.6 69.6 %all-to-all-start = ((bf16[4,256,1024]{2,1,0:T(8,128)(2,1)}), bf16[4,256,1024]{2,1,0:T(8,128)(2,1)S(1)}, u32[]{:S(2)}, u32[]{:S(2)}) async-start(bf16[4,256,1024]{2,1,0:T(8,128)(2,1)} %constant_dynamic-slice_fusion.2), calls=%async_computation | async-start | bytes 4194304 | tf_op jit(solution)/shard_map/all_to_all | solution.py:554
  89.2 34.0 %all-to-all-start.3 = ((bf16[4,256,1024]{2,1,0:T(8,128)(2,1)}), bf16[4,256,1024]{2,1,0:T(8,128)(2,1)}, u32[]{:S(2)}, u32[]{:S(2)}) async-start(bf16[4,256,1024]{2,1,0:T(8,128)(2,1)} %constant_dynamic-slice_fusion), calls=%async_computation.3 | async-start | bytes 4194304 | tf_op jit(solution)/shard_map/all_to_all | solution.py:554
  93.6 634.5 %all-reduce.4.cloned.1.call-start = ((), (), s32[]{:S(2)}) async-start(), calls=%async_computation.19 | async-start | bytes 262144
  94.6 38.1 %copy-start.13 = (f32[1024]{0:T(1024)}, f32[1024]{0:T(1024)S(1)}, u32[]{:S(2)}) copy-start(f32[1024]{0:T(1024)S(1)} %get-tuple-element.52) | copy-start | bytes 12292
  94.6 38.1 %copy-start.16 = (f32[1024]{0:T(1024)}, f32[1024]{0:T(1024)S(1)}, u32[]{:S(2)}) copy-start(f32[1024]{0:T(1024)S(1)} %get-tuple-element.51) | copy-start | bytes 12292
  94.6 219.0 %copy-start.20 = (f32[1024]{0:T(1024)}, f32[1024]{0:T(1024)S(1)}, u32[]{:S(2)}) copy-start(f32[1024]{0:T(1024)S(1)} %get-tuple-element.49) | copy-start | bytes 12292
  143.6 9.2 copy-start.11
  196.6 2.6 copy-start.3
  207.3 1.9 copy-start.9
  381.3 4.7 copy-start.8
  386.0 2.1 copy-start.6
  386.0 3.1 copy-start.10
  386.0 55.6 %slice-start = ((s8[6291456]{0:T(1024)(128)(4,1)}), s8[4194304]{0:T(1024)(128)(4,1)S(1)}, s32[]{:S(2)}) async-start(s8[6291456]{0:T(1024)(128)(4,1)} %bitcast.254), calls=%async_computation.20 | async-start | bytes 8388608
  389.1 2.4 copy-start.12
  389.1 52.5 %slice-start.1 = ((s8[6291456]{0:T(1024)(128)(4,1)}), s8[2097152]{0:T(1024)(128)(4,1)S(1)}, s32[]{:S(2)}) async-start(s8[6291456]{0:T(1024)(128)(4,1)} %bitcast.254), calls=%async_computation.21 | async-start | bytes 4194304
  441.7 8.5 copy-start.2
  451.8 5.4 copy-start.14
  451.8 5.4 copy-start.15
  457.3 4.3 copy-start.19
  457.3 4.7 copy-start.4
  457.3 5.9 copy-start.5
  463.2 2.2 copy-start.7
  463.2 2.2 copy-start.17
  465.4 4.3 copy-start.18
  470.5 261.9 %reduce-scatter.7.cloned.1.call-start = ((), (), s32[]{:S(2)}) async-start(), calls=%async_computation.12 | async-start | bytes 2162688 | tf_op jit(solution)/shard_map/reduce_scatter | solution.py:561
  476.7 374.1 %reduce-scatter.5.cloned.1.call-start = ((), (), s32[]{:S(2)}) async-start(), calls=%async_computation.11 | async-start | bytes 6488064 | tf_op jit(solution)/shard_map/reduce_scatter | solution.py:561
  496.7 0.7 copy-start.22
  496.8 504.5 %all-gather.12.cloned.1.call-start = ((), (), s32[]{:S(2)}) async-start(), calls=%async_computation.9 | async-start | bytes 10485760 | tf_op jit(solution)/shard_map/all_gather | solution.py:558
  584.3 566.4 %all-gather.14.cloned.1.call-start = ((), (), s32[]{:S(2)}) async-start(), calls=%async_computation.10 | async-start | bytes 10485760 | tf_op jit(solution)/shard_map/all_gather | solution.py:558
  655.3 681.6 %reduce-scatter.11.cloned.1.call-start = ((), (), s32[]{:S(2)}) async-start(), calls=%async_computation.14 | async-start | bytes 8650752 | tf_op jit(solution)/shard_map/reduce_scatter | solution.py:561
  687.3 0.7 copy-start.21
  687.4 835.9 %reduce-scatter.9.cloned.1.call-start = ((), (), s32[]{:S(2)}) async-start(), calls=%async_computation.13 | async-start | bytes 8650752 | tf_op jit(solution)/shard_map/reduce_scatter | solution.py:561
  1533.2 8.1 copy-start.1
Sparse Core Ops, SparseCore 0:
  11.0 59.5 all-gather.17
  74.1 69.4 all-gather.15
  146.6 76.1 all-gather.19
  225.6 75.8 all-gather.21
  470.6 121.2 all-reduce.3
  594.1 137.7 reduce-scatter.6
  738.4 112.3 reduce-scatter.4
  852.4 148.8 all-gather.11
  1002.8 147.8 all-gather.13
  1152.9 184.0 reduce-scatter.10
  1339.8 183.4 reduce-scatter.8

commit v2 on v1

--- a/solution.py
+++ b/solution.py
@@ -551,11 +551,18 @@
 
     def to_sequences(value):
         mine = lax.dynamic_slice_in_dim(value, place * per_group, per_group, axis=0)
-        return lax.all_to_all(mine, "ctx", split_axis=0, concat_axis=1, tiled=True)
+        mine = mine.reshape((ctxs, seqs) + value.shape[1:])
+        mine = lax.all_to_all(mine, "ctx", split_axis=0, concat_axis=0, tiled=True)
+        return jnp.swapaxes(mine, 0, 1)
 
     def to_spans(value):
-        mine = lax.all_to_all(value, "ctx", split_axis=1, concat_axis=0, tiled=True)
+        mine = jnp.swapaxes(value.reshape(seqs, ctxs, span, model), 0, 1)
+        mine = lax.all_to_all(mine, "ctx", split_axis=0, concat_axis=0, tiled=True)
+        mine = mine.reshape(per_group, span, model)
         return lax.all_gather(mine, "tensor", axis=0, tiled=True)
+
+    def by_owner(value, columns):
+        return value.reshape(owners, shard, groups, columns).transpose(0, 2, 1, 3)
 
     def scatter(value):
         return lax.psum_scatter(value, ALL, scatter_dimension=0, tiled=True)
@@ -573,7 +580,14 @@
             up_bias.reshape(-1),
         ]
     )
-    small = gather(small)
+    first_pack = jnp.concatenate([w_query, w_key, w_value, w_out.T], axis=1)
+    pack_width = first_pack.shape[1]
+    extra = -(-small.shape[0] // (16 * pack_width)) * 16
+    small = jnp.pad(small, (0, extra * pack_width - small.shape[0])).reshape(extra, pack_width)
+    first_pack = gather(jnp.concatenate([first_pack, small], axis=0))
+    small = first_pack[:, :, shard:].reshape(owners, groups, extra * pack_width)
+    first_pack = first_pack[:, :, :shard]
+    second_pack = gather(jnp.stack([w_up, w_down.T]))
     vectors = small[:, 0, : 6 * shard].reshape(owners, 6, shard).transpose(1, 0, 2)
     vectors = vectors.reshape(6, model).astype(jnp.float32)
     gain_one, shift_one, bias_out, gain_two, shift_two, bias_down = (
@@ -591,11 +605,11 @@
     bias_up = heads_bias(bias_first + 2 * heads * shared, shared_up).reshape(-1)
     bias_qkv = jnp.stack([bias_query, jnp.zeros_like(bias_query), bias_value], axis=1).reshape(-1)
 
-    full_qkv = gather(jnp.concatenate([w_query, w_key, w_value], axis=1))
-    full_qkv = full_qkv.transpose(0, 2, 1, 3).reshape(model, groups * 3 * width)
-    full_out = gather(w_out).transpose(1, 2, 0, 3).reshape(groups * width, model)
-    full_up = gather(w_up).transpose(0, 2, 1, 3).reshape(model, groups * hidden)
-    full_down = gather(w_down).transpose(1, 2, 0, 3).reshape(groups * hidden, model)
+    full_qkv = first_pack[..., : 3 * width].transpose(0, 2, 1, 3)
+    full_qkv = full_qkv.reshape(model, groups * 3 * width)
+    turned_out = first_pack[..., 3 * width :].transpose(0, 2, 1, 3).reshape(model, groups * width)
+    full_up = second_pack[:, :, 0].transpose(0, 2, 1, 3).reshape(model, groups * hidden)
+    turned_down = second_pack[:, :, 1].transpose(0, 2, 1, 3).reshape(model, groups * hidden)
 
     inputs_low = to_sequences(tokens)
     segs = to_sequences(segment_ids)
@@ -610,33 +624,32 @@
     qkv = qkv.reshape(seqs, length, groups * 3 * width)
     mixed, log_total = attend(slopes, seg_row, seg_col, qkv, groups, heads)
     mixed = mixed.reshape(rows, groups * width)
-    residual = inputs + matmul(mixed, full_out) + bias_out
+    residual = inputs + matmul_right(mixed, turned_out) + bias_out
     normed_two = layer_norm(residual, gain_two, shift_two).astype(jnp.bfloat16)
     pre_act = matmul(normed_two, full_up) + bias_up
     activated = gelu_tanh(pre_act).astype(jnp.bfloat16)
-    result = (residual + matmul(activated, full_down) + bias_down).astype(jnp.bfloat16)
+    result = (residual + matmul_right(activated, turned_down) + bias_down).astype(jnp.bfloat16)
     outputs = to_spans(result.reshape(seqs, length, model))
 
-    act_grad = matmul_right(cotangent, full_down)
+    act_grad = matmul(cotangent, turned_down)
     unused, gelu_pull = jax.vjp(gelu_tanh, pre_act)
     pre_grad = gelu_pull(act_grad)[0].astype(jnp.bfloat16)
-    grad_down = matmul_left(activated, cotangent)
-    grad_down = grad_down.reshape(groups, hidden, owners, shard).transpose(2, 0, 1, 3)
-    sum_down = scatter(grad_down.astype(jnp.bfloat16).reshape(-1, shard)).astype(jnp.float32)
+    grad_down = matmul_left(cotangent, activated).astype(jnp.bfloat16)
     grad_ubias = jnp.sum(pre_grad.astype(jnp.float32), axis=0)
-    grad_up = matmul_left(normed_two, pre_grad)
-    grad_up = grad_up.reshape(owners, shard, groups, hidden).transpose(0, 2, 1, 3)
-    sum_up = scatter(grad_up.astype(jnp.bfloat16).reshape(-1, hidden)).astype(jnp.float32)
+    grad_up = matmul_left(normed_two, pre_grad).astype(jnp.bfloat16)
+    grad_ff = jnp.stack([by_owner(grad_up, hidden), by_owner(grad_down, hidden)], axis=2)
+    grad_ff, outputs = lax.optimization_barrier((grad_ff, outputs))
+    sum_ff = scatter(grad_ff.reshape(-1, hidden)).astype(jnp.float32)
+    sum_up = sum_ff[:shard]
+    sum_down = sum_ff[shard:].T
     normed_two_back = matmul_right(pre_grad, full_up)
     unused, norm_pull = jax.vjp(layer_norm, residual, gain_two, shift_two)
     resid_grad, gain_two_grad, shift_two_grad = norm_pull(normed_two_back)
     cot_rows = cotangent.astype(jnp.float32)
     resid_grad = resid_grad + cot_rows
     attn_grad = resid_grad.astype(jnp.bfloat16)
-    mixed_grad = matmul_right(attn_grad, full_out).astype(jnp.bfloat16)
-    grad_wout = matmul_left(mixed, attn_grad)
-    grad_wout = grad_wout.reshape(groups, width, owners, shard).transpose(2, 0, 1, 3)
-    sum_wout = scatter(grad_wout.astype(jnp.bfloat16).reshape(-1, shard)).astype(jnp.float32)
+    mixed_grad = matmul(attn_grad, turned_out).astype(jnp.bfloat16)
+    grad_wout = matmul_left(attn_grad, mixed).astype(jnp.bfloat16)
     qkv_grad = attend_back(
         slopes,
         seg_row,
@@ -652,9 +665,10 @@
     input_grad, gain_one_grad, shift_one_grad = first_pull(normed_one_back)
     input_grad = (input_grad + resid_grad).astype(jnp.bfloat16)
     tokens_grad = to_spans(input_grad.reshape(seqs, length, model))
-    grad_qkv = matmul_left(normed_one, qkv_grad)
-    grad_qkv = grad_qkv.reshape(owners, shard, groups, 3 * width).transpose(0, 2, 1, 3)
-    sum_qkv = scatter(grad_qkv.astype(jnp.bfloat16).reshape(-1, 3 * width)).astype(jnp.float32)
+    grad_qkv = matmul_left(normed_one, qkv_grad).astype(jnp.bfloat16)
+    grad_pack = jnp.concatenate(
+        [by_owner(grad_qkv, 3 * width), by_owner(grad_wout, width)], axis=3
+    )
     grad_bias = jnp.sum(qkv_grad.astype(jnp.float32), axis=0).reshape(groups, 3, heads, HEAD_DIM)
 
     grad_vectors = jnp.stack(
@@ -685,7 +699,15 @@
         ],
         axis=2,
     )
-    sum_small = scatter(grad_small.reshape(owners * groups, -1))[0]
+    grad_small = grad_small.astype(jnp.bfloat16)
+    padding = extra * pack_width - grad_small.shape[2]
+    grad_small = jnp.pad(grad_small, ((0, 0), (0, 0), (0, padding)))
+    grad_small = grad_small.reshape(owners, groups, extra, pack_width)
+    grad_pack = jnp.concatenate([grad_pack, grad_small], axis=2)
+    sum_pack = scatter(grad_pack.reshape(-1, pack_width)).astype(jnp.float32)
+    sum_small = sum_pack[shard:].reshape(-1)
+    sum_qkv = sum_pack[:shard, : 3 * width]
+    sum_wout = sum_pack[:shard, 3 * width :].T
     sums = sum_small[: 6 * shard].reshape(6, shard)
     sum_biases = sum_small[6 * shard :]
     count = heads * shared
@@ -704,7 +726,7 @@
         sums[3],
         sums[4],
         sum_up,
-        sum_biases[2 * count :].reshape(heads, shared_up),
+        sum_biases[2 * count : 2 * count + heads * shared_up].reshape(heads, shared_up),
         sum_down,
         sums[5],
     )

time: 1560 us -> 1190 us (0.76)
  waiting for transfers between devices: 898 us -> 576 us
  blocking collectives: 124 us -> 29 us
  local copies, waits for them, and re-layouts: 200 us -> 248 us
    all_gather x2, waiting for transfers between devices: 298 us -> 99.5 us  [to_spans(): return lax.all_gather(mine, 'tensor', axis=0, tiled=True)]
    reduce_scatter x4 -> x2, waiting for transfers between devices: 488 us -> 365 us  [scatter(): return lax.psum_scatter(value, ALL, scatter_dimension=0, tiled=True)]
    unnamed x1 -> x0, blocking collectives: 61.4 us -> none
    optimization_barrier x0 -> x1, local copies, waits for them, and re-layouts: none -> 44.8 us  [whole_sequences(): grad_ff, outputs = lax.optimization_barrier((grad_ff, outputs))]
    all_to_all x3 -> x4, waiting for transfers between devices: 26.6 us -> 67.5 us  [the longest x3 67.5 us: to_sequences(): mine = lax.all_to_all(mine, 'ctx', split_axis=0, concat_axis=0, tiled=True)]
    all_gather x4 -> x2, waiting for transfers between devices: 83.4 us -> 44.1 us  [gather(): whole = lax.all_gather(value, ALL, axis=0, tiled=False)]
    convert_element_type x5 -> x0, local copies, waits for them, and re-layouts: 36.6 us -> none  [the longest x2 24.5 us: whole_sequences(): grad_up.astype(jnp.bfloat16).reshape(-1, hidden)]
    all_to_all x2 -> x1, blocking collectives: 63.1 us -> 29 us  [to_spans(): mine = lax.all_to_all(mine, 'ctx', split_axis=0, concat_axis=0, tiled=True)]
  transfers between devices with their start and end apart: 14 -> 10, of which waited for: 10 -> 7; matrix products, arithmetic and copies ran while one was open for 18% -> 29% of each run, Pallas kernels for 2% -> 7%
where the time goes in v2:
time: 1190 us; the launch traced here: 1170 us
  waiting for transfers between devices  576 us (48%)
  local copies, waits for them, and re-layouts  248 us (21%)
  matrix products  155 us (13%)
  Pallas kernels  84.1 us (7%)
  other arithmetic  49.2 us (4%)
  blocking collectives  29 us (2%)
  starting transfers between devices  17.1 us (1%)
  between operations  15.2 us (1%)
    reduce_scatter x2, waiting for transfers between devices, scatter(): return lax.psum_scatter(value, ALL, scatter_dimension=0, tiled=True)  365 us
    all_gather x2, waiting for transfers between devices, to_spans(): return lax.all_gather(mine, 'tensor', axis=0, tiled=True)  99.5 us
    all_to_all x3, waiting for transfers between devices, to_sequences(): mine = lax.all_to_all(mine, 'ctx', split_axis=0, concat_axis=0, tiled=True)  67.5 us
    dot_general x4, matrix products, matmul(): return jnp.dot(left, right, preferred_element_type=jnp.float32)  60.3 us
    unnamed x63, local copies, waits for them, and re-layouts  56.2 us
    reshape x6, local copies, waits for them, and re-layouts, by_owner(): return value.reshape(owners, shard, groups, columns).transpose(0, 2, 1, 3)  53.5 us
    pallas_call x1, Pallas kernels, attend_back(): pl.pallas_call(functools.partial(attend_back_kernel, heads, block), grid=...  50.3 us
    dot_general x4, matrix products, matmul_right(): lax.dot_general(left, right, (((1,), (1,)), ((), ())), preferred_element_...  47.1 us
  transfers between devices with their start and end apart: 10, of which 7 were waited for; matrix products, arithmetic and copies ran while one was open for 29% of the time, Pallas kernels for 7%

profile of v2, /device:TPU:0, one launch (start us, length us, event | category | flops | bytes accessed | tf_op | source)
XLA Modules:
  0.0 1173.3 jit_solution(5401483107789454571)
XLA Ops:
  9.5 4.1 concatenate.21
  14.6 1.6 pad_maximum_fusion.3
  17.4 1.8 pad_maximum_fusion.2
  19.9 4.2 all-to-all-start.1
  24.1 3.1 dynamic-slice_bitcast_fusion.1
  27.9 3.6 all-to-all-start
  31.5 3.1 dynamic-slice_bitcast_fusion
  34.6 26.8 %all-to-all-done = bf16[4,1,256,1024]{3,2,1,0:T(8,128)(2,1)S(1)} async-done(((bf16[4,1,256,1024]{3,2,1,0:T(8,128)(2,1)}), bf16[4,1,256,1024]{3,2,1,0:T(8,128)(2,1)S(1)}, u32[]{:S(2)}, u32[]{:S(2)}) %all-to-all-start) | async-done | bytes 2097184 | tf_op jit(solution)/shard_map/all_to_all | solution.py:555
  61.4 4.5 all-to-all-start.2
  68.5 40.0 %all-to-all-done.2 = bf16[4,1,256,1024]{3,2,1,0:T(8,128)(2,1)} async-done(((bf16[4,1,256,1024]{3,2,1,0:T(8,128)(2,1)}), bf16[4,1,256,1024]{3,2,1,0:T(8,128)(2,1)}, u32[]{:S(2)}, u32[]{:S(2)}) %all-to-all-start.2) | async-done | bytes 2097184 | tf_op jit(solution)/shard_map/all_to_all | solution.py:555
  108.5 2.5 convert_reduce_fusion.1
  111.0 9.0 all-gather.9.cloned.1.call-done
  120.0 2.3 slice.173
  122.3 2.6 reshape.420
  128.2 6.5 slice_bitcast_fusion
  134.7 9.1 copy.90
  143.8 3.2 slice_bitcast_fusion.1
  147.0 4.3 copy.95
  152.2 10.5 fusion.20.qkv_ref
  162.7 33.8 %attend.1 = (bf16[1,1024,1024]{2,1,0:T(8,128)(2,1)S(1)}, f32[1,4,4,1024]{3,2,1,0:T(4,128)S(1)}) custom-call(f32[16]{0:T(128)S(1)} %multiply_exponential_fusion.slope_ref, s32[1,1,1024]{2,1,0:T(1,128)S(1)} %bitcast.234, s32[1,1024,1]{2,1,0:T(8,128)S(1)} %copy.94.col_ref, bf16[1,1024,3072]{2,1,0:T(8,128)(2,1)S(1)} %fusion.20.qkv_ref), custom_call_target="tpu_custom_call" | custom-call | tf_op jit(solution)/shard_map/attend/pallas_call | solution.py:480
  196.6 2.5 fusion.91
  199.1 2.1 copy-done.7
  201.7 35.1 %all-gather.11.cloned.1.call-done = bf16[64,128,1024]{2,1,0:T(8,128)(2,1)} async-done(((bf16[2,128,1024]{2,1,0:T(8,128)(2,1)}), bf16[64,128,1024]{2,1,0:T(8,128)(2,1)}) %all-gather.11.cloned.1.call-update) | async-done | bytes 16777232 | tf_op jit(solution)/shard_map/all_gather | solution.py:549
  236.9 12.0 %fusion.85 = (bf16[8,4,1,128,1024]{4,3,2,1,0:T(8,128)(2,1)}, bf16[8,4,1,128,1024]{4,3,2,1,0:T(8,128)(2,1)}) fusion(bf16[8,4,2,128,1024]{4,3,2,1,0:T(8,128)(2,1)} %bitcast.240), kind=kLoop, calls=%fused_computation.138 | loop fusion | bytes 33554432 | tf_op jit(solution)/shard_map/slice | solution.py:612
  248.9 12.4 %copy.126 = bf16[8,4,1,128,1024]{3,0,4,1,2:T(8,128)(2,1)} copy(bf16[8,4,1,128,1024]{4,3,2,1,0:T(8,128)(2,1)} %get-tuple-element.104) | data formatting | bytes 16777216
  261.3 12.4 %copy.124 = bf16[8,4,1,128,1024]{3,0,4,1,2:T(8,128)(2,1)} copy(bf16[8,4,1,128,1024]{4,3,2,1,0:T(8,128)(2,1)} %get-tuple-element.105) | data formatting | bytes 16777216
  273.7 17.2 %fusion.12 = f32[1024,4096]{1,0:T(8,128)} fusion(bf16[512,8,8,128]{3,2,1,0:T(8,128)(2,1)} %bitcast.247, f32[1024,1024]{1,0:T(8,128)} %copy-done.7, f32[1024]{0:T(1024)S(1)} %get-tuple-element.120, f32[1024]{0:T(1024)S(1)} %get-tuple-element.121, f32[1024]{0:T(1024)S(1)} %fusion.77, f32[1024]{0:T(1024)S(1)} %broadcast_multiply_fusion), kind=kOutput, calls=%fused_computation.20 | convolution fusion | flops 8595177472 | bytes 29376512 | tf_op jit(solution)/shard_map/dot_general | solution.py:34
  290.9 18.1 %add_convert_fusion.2 = bf16[1024,1024]{1,0:T(8,128)(2,1)} fusion(f32[1024,1024]{1,0:T(8,128)S(1)} %copy-done.8, bf16[512,8,8,128]{3,2,1,0:T(8,128)(2,1)} %bitcast.249, f32[1024]{0:T(1024)S(1)} %get-tuple-element.119, f32[1024,4096]{1,0:T(8,128)} %fusion.12, f32[4096]{0:T(1024)S(1)} %reshape.407), kind=kOutput, calls=%fused_computation.65 | convolution fusion | flops 8635023360 | bytes 31477760 | tf_op jit(solution)/shard_map/dot_general | solution.py:44
  309.0 4.5 all-to-all-start.3
  313.6 28.6 %fusion.92 = (bf16[4096]{0:T(1024)(128)(2,1)S(1)}, bf16[1024,4096]{1,0:T(8,128)(2,1)}) fusion(bf16[1024,1024]{1,0:T(8,128)(2,1)} %bitcast.29, bf16[512,8,8,128]{3,2,1,0:T(8,128)(2,1)} %bitcast.250, f32[1024,4096]{1,0:T(8,128)} %fusion.12, f32[4096]{0:T(1024)S(1)} %reshape.407), kind=kOutput, calls=%fused_computation.145 | convolution fusion | flops 8698982400 | bytes 35676160 | tf_op jit(solution)/shard_map/dot_general | solution.py:34
  342.3 15.5 %multiply_reduce_fusion = (bf16[1024]{0:T(1024)(128)(2,1)S(1)}, f32[1024]{0:T(1024)S(1)}, bf16[1024]{0:T(1024)(128)(2,1)S(1)}, f32[1024,1024]{1,0:T(8,128)S(1)}) fusion(f32[1024,1024]{1,0:T(8,128)} %copy-done.7, f32[1024]{0:T(1024)S(1)} %fusion.77, f32[1024]{0:T(1024)S(1)} %broadcast_multiply_fusion, f32[1024]{0:T(1024)S(1)} %get-tuple-element.121, ...), kind=kOutput, calls=%fused_computation.61 | convolution fusion | flops 8598320128 | bytes 25186304 | tf_op jit(solution)/shard_map/dot_general | solution.py:44
  357.8 1.8 fusion.84
  359.6 2.2 fusion.83
  361.8 2.1 copy-done.10
  363.9 3.8 fusion.61
  367.6 3.3 reshape.394
  371.0 1.7 copy.194
  372.8 1.2 copy-done.11
  374.0 4.0 convert_bitcast_fusion.do_ref
  377.9 50.3 %attend_back.1 = bf16[1,1024,3072]{2,1,0:T(8,128)(2,1)S(1)} custom-call(f32[16]{0:T(128)S(1)} %multiply_exponential_fusion.slope_ref, s32[1,1,1024]{2,1,0:T(1,128)S(1)} %bitcast.235, s32[1,1024,1]{2,1,0:T(8,128)S(1)} %copy.94.col_ref, bf16[1,1024,3072]{2,1,0:T(8,128)(2,1)} %copy-done.2, bf16[1,1024,1024]{2,1,0:T(8,128)(2,1)S(1)} %convert_bitcast_fusion.do_ref, ...), custom_call_target="tpu_custom_call" | custom-call | tf_op jit(solution)/shard_map/attend_back/pallas_call | solution.py:498
  428.3 2.7 copy-done.3
  431.0 3.9 reduce.6
  434.8 11.5 fusion.28
  446.3 12.3 %reshape.393 = bf16[8,128,4,768]{3,2,1,0:T(4,128)(2,1)} reshape(bf16[1024,3072]{1,0:T(8,128)(2,1)} %fusion.28) | data formatting | bytes 12582912 | tf_op jit(solution)/shard_map/reshape | solution.py:565
  458.6 6.8 copy.193
  466.2 11.0 fusion.82
  477.2 2.0 copy-done.12
  479.2 2.4 fusion.46
  482.9 1.8 reshape.400
  484.7 7.6 pad_maximum_fusion.1
  492.4 4.3 add_convert_fusion.1
  496.7 29.0 %all_to_all.25 = bf16[4,1,256,1024]{3,2,1,0:T(8,128)(2,1)} all-to-all(bf16[4,1,256,1024]{3,2,1,0:T(8,128)(2,1)S(1)} %bitcast.251), channel_id=1, replica_groups=mesh['dp'=2,'ctx'=4,'tensor'=4] {'ctx'}, dimensions={0} | all-to-all | bytes 4194304 | tf_op jit(solution)/shard_map/all_to_all | solution.py:560
  525.8 16.2 %convolution_convert_fusion = bf16[1024,4096]{1,0:T(8,128)(2,1)} fusion(bf16[1024,1024]{1,0:T(8,128)(2,1)} %bitcast.29, f32[1024,4096]{1,0:T(8,128)} %fusion.12, f32[4096]{0:T(1024)S(1)} %reshape.407), kind=kOutput, calls=%fused_computation.22 | convolution fusion | flops 8636071936 | bytes 27279360 | tf_op jit(solution)/shard_map/dot_general | solution.py:38
  542.0 14.6 %reshape.388 = bf16[8,128,4,1024]{3,2,1,0:T(4,128)(2,1)} reshape(bf16[1024,4096]{1,0:T(8,128)(2,1)} %convolution_convert_fusion) | data formatting | bytes 16777216 | tf_op jit(solution)/shard_map/reshape | solution.py:565
  556.6 15.6 %convolution_convert_fusion.1 = bf16[1024,4096]{1,0:T(8,128)(2,1)} fusion(bf16[1024,4096]{1,0:T(8,128)(2,1)} %get-tuple-element.138, f32[1024,1024]{1,0:T(8,128)} %copy-done.7, f32[1024]{0:T(1024)S(1)} %copy-done.22, f32[1024]{0:T(1024)S(1)} %get-tuple-element.121, f32[1024]{0:T(1024)S(1)} %fusion.77, f32[1024]{0:T(1024)S(1)} %broadcast_multiply_fusion), kind=kOutput, calls=%fused_computation.23 | convolution fusion | flops 8599371776 | bytes 20987904 | tf_op jit(solution)/shard_map/dot_general | solution.py:38
  572.2 14.6 %reshape.387 = bf16[8,128,4,1024]{3,2,1,0:T(4,128)(2,1)} reshape(bf16[1024,4096]{1,0:T(8,128)(2,1)} %convolution_convert_fusion.1) | data formatting | bytes 16777216 | tf_op jit(solution)/shard_map/reshape | solution.py:565
  586.9 15.2 %pad_maximum_fusion = bf16[8,4,2,128,1024]{4,1,3,0,2:T(4,128)(2,1)} fusion(bf16[8,4,1,128,1024]{4,1,3,0,2:T(4,128)(2,1)} %bitcast.237, bf16[8,4,1,128,1024]{4,1,3,0,2:T(4,128)(2,1)} %bitcast.238), kind=kLoop, calls=%fused_computation.10 | loop fusion | flops 8388608 | bytes 33554432 | tf_op jit(solution)/shard_map/stack | solution.py:640
  602.1 44.8 %copy.111 = bf16[8,4,2,128,1024]{3,2,1,0,4:T(2,128)(2,1)} copy(bf16[8,4,2,128,1024]{4,1,3,0,2:T(4,128)(2,1)} %pad_maximum_fusion) | data formatting | bytes 33554432 | tf_op jit(solution)/shard_map/optimization_barrier | solution.py:641
  646.9 28.0 %reshape.403 = bf16[8192,1024]{0,1:T(8,128)(2,1)} reshape(bf16[8,4,2,128,1024]{3,2,1,0,4:T(2,128)(2,1)} %copy.111) | data formatting | bytes 33554432 | tf_op jit(solution)/shard_map/reshape | solution.py:642
  679.9 1.7 fusion.88
  681.6 99.5 %all-gather.15.cloned.1.call-done = bf16[16,1,256,1024]{3,2,1,0:T(8,128)(2,1)} async-done(((bf16[4,1,256,1024]{3,2,1,0:T(8,128)(2,1)}), bf16[16,1,256,1024]{3,2,1,0:T(8,128)(2,1)}) %all-gather.15.cloned.1.call-update) | async-done | bytes 8388624 | tf_op jit(solution)/shard_map/all_gather | solution.py:562
  781.1 364.7 %reduce-scatter.5.cloned.1.call-done = bf16[256,1024]{0,1:T(8,128)(2,1)} async-done(((bf16[8192,1024]{0,1:T(8,128)(2,1)}), bf16[256,1024]{0,1:T(8,128)(2,1)}) %reduce-scatter.5.cloned.1.call-update) | async-done | bytes 524304 | tf_op jit(solution)/shard_map/reduce_scatter | solution.py:568
  1149.8 8.1 copy.205
  1157.9 8.1 copy.206
  (136 shorter events, 24.1 us)
Async XLA Ops:
  7.2 12.1 %copy-start = (s32[16,256]{1,0:T(8,128)S(1)}, s32[16,256]{1,0:T(8,128)}, u32[]{:S(2)}) copy-start(s32[16,256]{1,0:T(8,128)} %param.19) | copy-start | bytes 49156
  7.2 112.8 %all-gather.9.cloned.1.call-start = ((), (), s32[]{:S(2)}) async-start(), calls=%async_computation.9 | async-start | bytes 9732096 | tf_op jit(solution)/shard_map/all_gather | solution.py:549
  16.3 220.6 %all-gather.11.cloned.1.call-start = ((), (), s32[]{:S(2)}) async-start(), calls=%async_computation.10 | async-start | bytes 17301504 | tf_op jit(solution)/shard_map/all_gather | solution.py:549
  19.9 8.0 all-to-all-start.1
  27.9 33.5 %all-to-all-start = ((bf16[4,1,256,1024]{3,2,1,0:T(8,128)(2,1)}), bf16[4,1,256,1024]{3,2,1,0:T(8,128)(2,1)S(1)}, u32[]{:S(2)}, u32[]{:S(2)}) async-start(bf16[4,1,256,1024]{3,2,1,0:T(8,128)(2,1)} %dynamic-slice_bitcast_fusion.1), calls=%async_computation | async-start | bytes 4194304 | tf_op jit(solution)/shard_map/all_to_all | solution.py:555
  61.4 89.9 %copy-start.4 = (bf16[4,1,256,1024]{3,2,1,0:T(8,128)(2,1)}, bf16[4,1,256,1024]{3,2,1,0:T(8,128)(2,1)S(1)}, u32[]{:S(2)}) copy-start(bf16[4,1,256,1024]{3,2,1,0:T(8,128)(2,1)S(1)} %all-to-all-done) | copy-start | bytes 6291460
  61.4 47.1 %all-to-all-start.2 = ((bf16[4,1,256,1024]{3,2,1,0:T(8,128)(2,1)}), bf16[4,1,256,1024]{3,2,1,0:T(8,128)(2,1)}, u32[]{:S(2)}, u32[]{:S(2)}) async-start(bf16[4,1,256,1024]{3,2,1,0:T(8,128)(2,1)} %dynamic-slice_bitcast_fusion), calls=%async_computation.2 | async-start | bytes 4194304 | tf_op jit(solution)/shard_map/all_to_all | solution.py:555
  151.3 11.4 copy-start.16
  151.3 122.4 %copy-start.21 = (f32[1024]{0:T(1024)}, f32[1024]{0:T(1024)S(1)}, u32[]{:S(2)}) copy-start(f32[1024]{0:T(1024)S(1)} %get-tuple-element.120) | copy-start | bytes 12292
  152.2 10.5 copy-start.14
  162.7 36.4 %copy-start.2 = (bf16[1,1024,3072]{2,1,0:T(8,128)(2,1)}, bf16[1,1024,3072]{2,1,0:T(8,128)(2,1)S(1)}, u32[]{:S(2)}) copy-start(bf16[1,1024,3072]{2,1,0:T(8,128)(2,1)S(1)} %fusion.20.qkv_ref) | copy-start | bytes 18874372
  162.7 33.9 %copy-start.5 = (bf16[4,1,256,1024]{3,2,1,0:T(8,128)(2,1)S(1)}, bf16[4,1,256,1024]{3,2,1,0:T(8,128)(2,1)}, u32[]{:S(2)}) copy-start(bf16[4,1,256,1024]{3,2,1,0:T(8,128)(2,1)} %copy-done.4) | copy-start | bytes 6291460
  162.7 33.9 %copy-start.13 = (bf16[8,128,4,256]{1,0,3,2:T(8,128)(2,1)S(1)}, bf16[8,128,4,256]{1,0,3,2:T(8,128)(2,1)}, u32[]{:S(2)}) copy-start(bf16[8,128,4,256]{1,0,3,2:T(8,128)(2,1)} %copy.95) | copy-start | bytes 6291460
  199.1 2.1 copy-start.7
  273.7 17.2 %copy-start.8 = (f32[1024,1024]{1,0:T(8,128)S(1)}, f32[1024,1024]{1,0:T(8,128)}, u32[]{:S(2)}) copy-start(f32[1024,1024]{1,0:T(8,128)} %copy-done.7) | copy-start | bytes 12582916
  309.0 33.2 %all-to-all-start.3 = ((bf16[4,1,256,1024]{3,2,1,0:T(8,128)(2,1)}), bf16[4,1,256,1024]{3,2,1,0:T(8,128)(2,1)}, u32[]{:S(2)}, u32[]{:S(2)}) async-start(bf16[4,1,256,1024]{3,2,1,0:T(8,128)(2,1)} %bitcast.258), calls=%async_computation.3 | async-start | bytes 4194304 | tf_op jit(solution)/shard_map/all_to_all | solution.py:560
  313.5 288.5 %all-gather.13.cloned.1.call-start = ((), (), s32[]{:S(2)}) async-start(), calls=%async_computation.11 | async-start | bytes 10485760 | tf_op jit(solution)/shard_map/all_gather | solution.py:562
  342.2 332.7 %reduce-scatter.3.cloned.1.call-start = ((), (), s32[]{:S(2)}) async-start(), calls=%async_computation.7 | async-start | bytes 9732096 | tf_op jit(solution)/shard_map/reduce_scatter | solution.py:568
  342.3 15.5 %copy-start.9 = (f32[1024,1024]{1,0:T(8,128)S(1)}, f32[1024,1024]{1,0:T(8,128)}, u32[]{:S(2)}) copy-start(f32[1024,1024]{1,0:T(8,128)} %copy-done.7) | copy-start | bytes 12582916
  361.8 2.1 copy-start.10
  371.0 3.0 copy-start.11
  428.3 2.7 copy-start.3
  431.0 3.9 copy-start.15
  458.6 7.5 copy-start.6
  458.6 7.5 copy-start.17
  458.6 7.5 copy-start.18
  466.2 11.1 copy-start.19
  477.2 2.0 copy-start.12
  477.2 4.5 copy-start.20
  492.3 288.8 %all-gather.15.cloned.1.call-start = ((), (), s32[]{:S(2)}) async-start(), calls=%async_computation.12 | async-start | bytes 10485760 | tf_op jit(solution)/shard_map/all_gather | solution.py:562
  525.7 620.1 %reduce-scatter.5.cloned.1.call-start = ((), (), s32[]{:S(2)}) async-start(), calls=%async_computation.8 | async-start | bytes 17301504 | tf_op jit(solution)/shard_map/reduce_scatter | solution.py:568
  542.0 14.6 %copy-start.22 = (f32[1024]{0:T(1024)S(1)}, f32[1024]{0:T(1024)}, u32[]{:S(2)}) copy-start(f32[1024]{0:T(1024)} %copy-done.21) | copy-start | bytes 12292
  1157.9 8.1 copy-start.1
Sparse Core Ops, SparseCore 0:
  16.4 103.5 all-gather.8
  123.6 113.2 all-gather.10
  342.3 148.9 all-gather.12
  497.0 133.8 reduce-scatter.2
  632.5 148.6 all-gather.14
  783.4 362.4 reduce-scatter.4
